TPU v7x, 256 devices: a whole 4x4x8 slice. The times are simulated.
256 devices in a mesh: illum: 4 (over x), gy: 16 (over y, z_lo, core), gx: 4 (over z_hi).
Axes of the slice: x: 4, y: 4, z: 8 (z_hi: 4, z_lo: 2; z = z_hi * 2 + z_lo), core: 2. Of those that a mesh axis runs over, the one named last changes fastest.
Arguments:
- incident: float32 [4, 2, 2048, 8192], P('illum', None, 'gy', 'gx'), may hold values from -6 to 6
- labels: int32 [2, 2048, 4, 4, 512], P(None, 'gy', 'gx', 'illum'), may hold values from 0 to 7
Outputs:
- exit_field: float32 [4, 2, 2048, 8192], P('illum', None, 'gy', 'gx')
- far_field: float32 [4, 2, 512, 512], P('illum', None, 'gy', 'gx')
Inputs may be any that keep to these rules, and one draw needn't show every extreme that they name: Material labels index the tables.
All inputs are finite; a program needn't handle non-finite values.
Results may differ from a plain program's by a relative error of at most 0.0003.
Values may be sent and summed in bfloat16 or wider, within the bound.
A program may use at most 64 MiB of HBM per device.

v0:
```python
import math

import jax
import jax.numpy as jnp
from jax import lax
from jax.sharding import PartitionSpec as P

SUB = 2
DET = 512


PHASE = (0.0, 0.03125, 0.0625, 0.09375, 0.125, 0.15625, 0.1875, 0.25)
DAMP = (1.0, 0.99609375, 0.9921875, 0.98828125, 0.984375, 0.9765625, 0.96875, 0.9375)
RATE = 0.24


def extended(block, sides, width):
    for axis, dim in sides:
        count = lax.axis_size(axis)
        forward = [(i, i + 1) for i in range(count - 1)]
        backward = [(target, source) for source, target in forward]
        low = lax.ppermute(
            lax.slice_in_dim(block, block.shape[dim] - width, None, axis=dim), axis, forward
        )
        high = lax.ppermute(lax.slice_in_dim(block, 0, width, axis=dim), axis, backward)
        block = jnp.concatenate([low, block, high], axis=dim)
    return block


def laplace(field):
    padded = jnp.pad(field, 1)
    return padded[:-2, 1:-1] + padded[2:, 1:-1] + padded[1:-1, :-2] + padded[1:-1, 2:] - 4.0 * field


def advance(pair, coefs):
    phase = coefs[0].astype(jnp.float32)
    damp = coefs[1].astype(jnp.float32)
    real = pair[0]
    imag = pair[1]
    real = damp * (real - (RATE * laplace(imag) + phase * imag))
    imag = damp * (imag + (RATE * laplace(real) + phase * real))
    return jnp.stack([real, imag])


def lookup(slab_labels, table):
    result = jnp.zeros(slab_labels.shape, jnp.float32)
    for number in range(len(table)):
        result = result + jnp.where(slab_labels == number, table[number], 0.0)
    return result.astype(jnp.bfloat16)


def on_device(incident, labels):
    rows = incident.shape[2]
    cols = incident.shape[3]
    field = incident[0]
    high = lax.Precision.HIGHEST
    for slab in range(labels.shape[0]):
        slab_labels = labels[slab]
        quarter = jnp.stack([lookup(slab_labels, PHASE), lookup(slab_labels, DAMP)])
        whole = lax.all_gather(quarter, "illum", axis=3, tiled=True)
        coefs = whole.reshape(2, rows, cols)
        coef_pad = extended(coefs, (("gy", 1), ("gx", 2)), 2)

        def thin_step(step, state):
            padded = extended(state, (("gy", 1), ("gx", 2)), 2)
            return advance(padded, coef_pad)[:, 2:-2, 2:-2]

        field = lax.fori_loop(0, SUB, thin_step, field)
    total_rows = lax.axis_size("gy") * rows
    total_cols = lax.axis_size("gx") * cols
    rows_pos = lax.axis_index("gy") * rows + jnp.arange(rows, dtype=jnp.int32)
    cols_pos = lax.axis_index("gx") * cols + jnp.arange(cols, dtype=jnp.int32)
    freqs = jnp.arange(DET, dtype=jnp.int32) - DET // 2
    angle_y = jnp.mod(freqs[:, None] * rows_pos[None, :], total_rows).astype(jnp.float32) * (
        2.0 * math.pi / total_rows
    )
    angle_x = jnp.mod(cols_pos[:, None] * freqs[None, :], total_cols).astype(jnp.float32) * (
        2.0 * math.pi / total_cols
    )
    cos_y, sin_y = (jnp.cos(angle_y), jnp.sin(angle_y))
    cos_x, sin_x = (jnp.cos(angle_x), jnp.sin(angle_x))
    scale = 1.0 / math.sqrt(total_rows * total_cols)
    real = field[0]
    imag = field[1]
    g_real = jnp.dot(real, cos_x, precision=high, preferred_element_type=jnp.float32) + jnp.dot(
        imag, sin_x, precision=high, preferred_element_type=jnp.float32
    )
    g_imag = jnp.dot(imag, cos_x, precision=high, preferred_element_type=jnp.float32) - jnp.dot(
        real, sin_x, precision=high, preferred_element_type=jnp.float32
    )
    f_real = jnp.dot(cos_y, g_real, precision=high, preferred_element_type=jnp.float32) + jnp.dot(
        sin_y, g_imag, precision=high, preferred_element_type=jnp.float32
    )
    f_imag = jnp.dot(cos_y, g_imag, precision=high, preferred_element_type=jnp.float32) - jnp.dot(
        sin_y, g_real, precision=high, preferred_element_type=jnp.float32
    )
    partial_far = jnp.stack([f_real, f_imag])
    by_rows = lax.psum_scatter(partial_far, "gy", scatter_dimension=1, tiled=True)
    far = lax.psum_scatter(by_rows, "gx", scatter_dimension=2, tiled=True)
    return (field[None], (far * scale)[None])


def solution(mesh):
    in_specs = (P("illum", None, "gy", "gx"), P(None, "gy", "gx", "illum", None))
    out_specs = (P("illum", None, "gy", "gx"), P("illum", None, "gy", "gx"))
    return jax.shard_map(
        on_device, mesh=mesh, in_specs=in_specs, out_specs=out_specs, check_vma=False
    )
```

profile of v0, /device:TPU:2, one launch (start us, length us, event | category | flops | bytes accessed | tf_op | source)
XLA Modules:
  0.0 435.2 jit_solution(3816574079993876474)
XLA Ops:
  11.4 27.2 %all-gather.5.cloned.1.call-done = bf16[2,128,1,4,512]{4,1,2,0,3:T(8,128)(2,1)} async-done(((bf16[2,128,1,1,512]{4,1,2,0,3:T(8,128)(2,1)}), bf16[2,128,1,4,512]{4,1,2,0,3:T(8,128)(2,1)}) %all-gather.5.cloned.1.call-update) | async-done | bytes 1048592 | tf_op jit(solution)/shard_map/all_gather | solution.py:60
  44.0 23.9 %all-gather.3.cloned.1.call-done = bf16[2,128,1,4,512]{4,1,2,0,3:T(8,128)(2,1)} async-done(((bf16[2,128,1,1,512]{4,1,2,0,3:T(8,128)(2,1)}), bf16[2,128,1,4,512]{4,1,2,0,3:T(8,128)(2,1)}) %all-gather.3.cloned.1.call-update) | async-done | bytes 1048592 | tf_op jit(solution)/shard_map/all_gather | solution.py:60
  77.4 2.4 pad_maximum_fusion.5
  81.2 4.4 %collective-permute-start.14 = (bf16[2,132,2]{1,2,0:T(2,128)(2,1)S(1)}, bf16[2,132,2]{1,2,0:T(2,128)(2,1)S(1)}, u32[]{:S(2)}, u32[]{:S(2)}) collective-permute-start(bf16[2,132,2]{1,2,0:T(2,128)(2,1)S(1)} %get-tuple-element.119), channel_id=1, source_target_pairs={{0,1},{1,2},{2,3},{4,5},{5,6},{6,7},{8,9},{9,10},{10,11},{12,13},{... | collective-permute-start | bytes 3176 | tf_op jit(solution)/shard_map/ppermute | solution.py:22
  90.5 6.3 %collective-permute-start.10 = (bf16[2,132,2]{1,2,0:T(2,128)(2,1)S(1)}, bf16[2,132,2]{1,2,0:T(2,128)(2,1)S(1)}, u32[]{:S(2)}, u32[]{:S(2)}) collective-permute-start(bf16[2,132,2]{1,2,0:T(2,128)(2,1)S(1)} %get-tuple-element.121), channel_id=1, source_target_pairs={{0,1},{1,2},{2,3},{4,5},{5,6},{6,7},{8,9},{9,10},{10,11},{12,13},{... | collective-permute-start | bytes 3176 | tf_op jit(solution)/shard_map/ppermute | solution.py:22
  98.8 9.5 %concatenate.39 = bf16[2,132,2052]{1,2,0:T(8,128)(2,1)S(1)} concatenate(bf16[2,132,2]{1,2,0:T(2,128)(2,1)S(1)} %collective-permute-done.14, bf16[2,132,2048]{1,2,0:T(8,128)(2,1)} %copy-done.5, bf16[2,132,2]{1,2,0:T(2,128)(2,1)S(1)} %collective-permute-done.15), dimensions={2} | concatenate | bytes 2166912 | tf_op jit(solution)/shard_map/concatenate | solution.py:26
  109.5 12.8 %concatenate.37 = bf16[2,132,2052]{1,2,0:T(8,128)(2,1)} concatenate(bf16[2,132,2]{1,2,0:T(2,128)(2,1)S(1)} %collective-permute-done.10, bf16[2,132,2048]{1,2,0:T(8,128)(2,1)} %copy-done.6, bf16[2,132,2]{1,2,0:T(2,128)(2,1)S(1)} %collective-permute-done.11), dimensions={2} | concatenate | bytes 2166912 | tf_op jit(solution)/shard_map/concatenate | solution.py:26
  122.2 3.8 copy.18
  126.1 59.4 %while.24 = (s32[]{:T(128)}, f32[2,128,2048]{2,1,0:T(8,128)S(1)}, bf16[2,132,2052]{2,1,0:T(8,128)(2,1)}, s32[]{:T(128)}) while((s32[]{:T(128)}, f32[2,128,2048]{2,1,0:T(8,128)S(1)}, bf16[2,132,2052]{2,1,0:T(8,128)(2,1)}, s32[]{:T(128)}) %tuple.90), condition=%wide.region_1.2_spmd, body=%wide.region_0.1_spmd.sunk | while | flops 8106370 | bytes 37169704 | solution.py:68
  127.4 4.0 collective-permute-start.1
  134.0 6.4 %collective-permute-start.2 = (f32[2,132,2]{2,1,0:T(8,128)S(1)}, f32[2,132,2]{2,1,0:T(8,128)S(1)}, u32[]{:S(2)}, u32[]{:S(2)}) collective-permute-start(f32[2,132,2]{2,1,0:T(8,128)S(1)} %get-tuple-element.179), channel_id=1, source_target_pairs={{0,1},{1,2},{2,3},{4,5},{5,6},{6,7},{8,9},{9,10},{10,11},{12,13},{... | collective-permute-start | bytes 6344 | tf_op jit(solution)/shard_map/while/body/eval_jaxpr/ppermute | solution.py:22
  143.6 5.7 %collective-permute-done.3 = f32[2,132,2]{2,1,0:T(8,128)} collective-permute-done((f32[2,132,2]{2,1,0:T(8,128)S(1)}, f32[2,132,2]{2,1,0:T(8,128)}, u32[]{:S(2)}, u32[]{:S(2)}) %collective-permute-start.3) | collective-permute-done | bytes 2144 | tf_op jit(solution)/shard_map/while/body/eval_jaxpr/ppermute | solution.py:25
  149.2 3.0 concatenate.42
  157.7 4.4 %collective-permute-start.1 = (f32[2,2,2048]{2,1,0:T(2,128)S(1)}, f32[2,2,2048]{2,1,0:T(2,128)S(1)}, u32[]{:S(2)}, u32[]{:S(2)}) collective-permute-start(f32[2,2,2048]{2,1,0:T(2,128)S(1)} %get-tuple-element.178), channel_id=1, source_target_pairs={{0,4},{4,8},{8,12},{12,16},{16,20},{20,24},{24,28},{28,32},{32,36}... | collective-permute-start | bytes 98312 | tf_op jit(solution)/shard_map/while/body/eval_jaxpr/ppermute | solution.py:22
  164.7 5.8 %collective-permute-start.2 = (f32[2,132,2]{2,1,0:T(8,128)S(1)}, f32[2,132,2]{2,1,0:T(8,128)S(1)}, u32[]{:S(2)}, u32[]{:S(2)}) collective-permute-start(f32[2,132,2]{2,1,0:T(8,128)S(1)} %get-tuple-element.179), channel_id=1, source_target_pairs={{0,1},{1,2},{2,3},{4,5},{5,6},{6,7},{8,9},{9,10},{10,11},{12,13},{... | collective-permute-start | bytes 6344 | tf_op jit(solution)/shard_map/while/body/eval_jaxpr/ppermute | solution.py:22
  173.7 4.7 %collective-permute-done.3 = f32[2,132,2]{2,1,0:T(8,128)} collective-permute-done((f32[2,132,2]{2,1,0:T(8,128)S(1)}, f32[2,132,2]{2,1,0:T(8,128)}, u32[]{:S(2)}, u32[]{:S(2)}) %collective-permute-start.3) | collective-permute-done | bytes 2144 | tf_op jit(solution)/shard_map/while/body/eval_jaxpr/ppermute | solution.py:25
  178.4 3.0 concatenate.42
  185.5 54.9 %while.25 = (s32[]{:T(128)}, f32[2,128,2048]{2,1,0:T(8,128)S(1)}, bf16[2,132,2052]{2,1,0:T(8,128)(2,1)S(1)}, s32[]{:T(128)}) while((s32[]{:T(128)}, f32[2,128,2048]{2,1,0:T(8,128)S(1)}, bf16[2,132,2052]{2,1,0:T(8,128)(2,1)S(1)}, s32[]{:T(128)}) %tuple.79), condition=%wide.region_3.4_spmd, body=%wide.region_2.3_spmd.sunk | while | flops 8106370 | bytes 32835852 | solution.py:68
  186.8 6.2 %collective-permute-start.5 = (f32[2,2,2048]{2,1,0:T(2,128)S(1)}, f32[2,2,2048]{2,1,0:T(2,128)S(1)}, u32[]{:S(2)}, u32[]{:S(2)}) collective-permute-start(f32[2,2,2048]{2,1,0:T(2,128)S(1)} %get-tuple-element.185), channel_id=1, source_target_pairs={{0,4},{4,8},{8,12},{12,16},{16,20},{20,24},{24,28},{28,32},{32,36}... | collective-permute-start | bytes 98312 | tf_op jit(solution)/shard_map/while/body/eval_jaxpr/ppermute | solution.py:22
  195.6 3.4 collective-permute-start.6
  202.3 4.7 %collective-permute-done.7 = f32[2,132,2]{2,1,0:T(8,128)} collective-permute-done((f32[2,132,2]{2,1,0:T(8,128)S(1)}, f32[2,132,2]{2,1,0:T(8,128)}, u32[]{:S(2)}, u32[]{:S(2)}) %collective-permute-start.7) | collective-permute-done | bytes 2144 | tf_op jit(solution)/shard_map/while/body/eval_jaxpr/ppermute | solution.py:25
  207.0 3.0 concatenate.43
  214.3 5.8 %collective-permute-start.5 = (f32[2,2,2048]{2,1,0:T(2,128)S(1)}, f32[2,2,2048]{2,1,0:T(2,128)S(1)}, u32[]{:S(2)}, u32[]{:S(2)}) collective-permute-start(f32[2,2,2048]{2,1,0:T(2,128)S(1)} %get-tuple-element.185), channel_id=1, source_target_pairs={{0,4},{4,8},{8,12},{12,16},{16,20},{20,24},{24,28},{28,32},{32,36}... | collective-permute-start | bytes 98312 | tf_op jit(solution)/shard_map/while/body/eval_jaxpr/ppermute | solution.py:22
  222.6 3.4 collective-permute-start.6
  229.3 4.8 %collective-permute-done.7 = f32[2,132,2]{2,1,0:T(8,128)} collective-permute-done((f32[2,132,2]{2,1,0:T(8,128)S(1)}, f32[2,132,2]{2,1,0:T(8,128)}, u32[]{:S(2)}, u32[]{:S(2)}) %collective-permute-start.7) | collective-permute-done | bytes 2144 | tf_op jit(solution)/shard_map/while/body/eval_jaxpr/ppermute | solution.py:25
  234.1 3.0 concatenate.43
  240.4 18.6 %fusion.21 = f32[128,512]{1,0:T(8,128)S(1)} fusion(s32[512]{0:T(512)S(1)} %iota_add_fusion.1, s32[2048]{0:T(1024)} %iota_add_fusion, f32[2,128,2048]{2,1,0:T(8,128)S(1)} %get-tuple-element.85), kind=kOutput, calls=%fused_computation.52 | convolution fusion | flops 1625292800 | bytes 1320960 | tf_op jit(solution)/shard_map/dot_general | solution.py:85
  259.0 18.3 %fusion.19 = f32[128,512]{1,0:T(8,128)S(1)} fusion(s32[512]{0:T(512)S(1)} %iota_add_fusion.1, s32[2048]{0:T(1024)S(1)} %copy-done.11, f32[2,128,2048]{2,1,0:T(8,128)S(1)} %get-tuple-element.85), kind=kOutput, calls=%fused_computation.51 | convolution fusion | flops 1625292800 | bytes 1320960 | tf_op jit(solution)/shard_map/dot_general | solution.py:88
  277.3 18.0 %fusion.29 = f32[128,512]{1,0:T(8,128)S(1)} fusion(f32[128,512]{1,0:T(8,128)S(1)} %fusion.21, s32[512]{0:T(512)S(1)} %iota_add_fusion.1, s32[2048]{0:T(1024)S(1)} %copy-done.11, f32[2,128,2048]{2,1,0:T(8,128)S(1)} %get-tuple-element.85), kind=kOutput, calls=%fused_computation.59 | convolution fusion | flops 1625358336 | bytes 1583104 | tf_op jit(solution)/shard_map/dot_general | solution.py:85
  295.3 18.3 %fusion.32 = f32[128,512]{1,0:T(8,128)S(1)} fusion(f32[128,512]{1,0:T(8,128)S(1)} %fusion.19, s32[512]{0:T(512)S(1)} %iota_add_fusion.1, s32[2048]{0:T(1024)S(1)} %copy-done.11, f32[2,128,2048]{2,1,0:T(8,128)S(1)} %get-tuple-element.85), kind=kOutput, calls=%fused_computation.60 | convolution fusion | flops 1625358336 | bytes 1583104 | tf_op jit(solution)/shard_map/dot_general | solution.py:88
  323.0 78.4 %reduce-scatter.3.cloned.1.call-done = f32[2,32,512]{2,1,0:T(8,128)} async-done(((f32[2,512,512]{2,1,0:T(8,128)}), f32[2,32,512]{2,1,0:T(8,128)}) %reduce-scatter.3.cloned.1.call-update) | async-done | bytes 131088 | tf_op jit(solution)/shard_map/reduce_scatter | solution.py:98
  401.4 25.5 %reduce-scatter.5.cloned.1.call-done = f32[2,32,128]{2,1,0:T(8,128)} async-done(((f32[2,32,512]{2,1,0:T(8,128)}), f32[2,32,128]{2,1,0:T(8,128)}) %reduce-scatter.5.cloned.1.call-update) | async-done | bytes 32784 | tf_op jit(solution)/shard_map/reduce_scatter | solution.py:99
  (133 shorter events, 81.3 us)
Async XLA Ops:
  7.2 31.5 %all-gather.5.cloned.1.call-start = ((), (), s32[]{:S(2)}) async-start(), calls=%async_computation.3 | async-start | bytes 1310720 | tf_op jit(solution)/shard_map/all_gather | solution.py:60
  10.0 58.0 %all-gather.3.cloned.1.call-start = ((), (), s32[]{:S(2)}) async-start(), calls=%async_computation.2 | async-start | bytes 1310720 | tf_op jit(solution)/shard_map/all_gather | solution.py:60
  10.8 390.6 %reduce-scatter.3.cloned.1.call-start = ((), (), s32[]{:S(2)}) async-start(), calls=%async_computation.4 | async-start | bytes 2228224 | tf_op jit(solution)/shard_map/reduce_scatter | solution.py:98
  41.1 34.4 %collective-permute-start.12 = (bf16[2,2,2048]{2,1,0:T(2,128)(2,1)S(1)}, bf16[2,2,2048]{2,1,0:T(2,128)(2,1)S(1)}, u32[]{:S(2)}, u32[]{:S(2)}) collective-permute-start(bf16[2,2,2048]{2,1,0:T(2,128)(2,1)S(1)} %copy.21), channel_id=1, source_target_pairs={{0,4},{4,8},{8,12},{12,16},{16,20},{20,24},{24,28},{28,32},{32,36}... | collective-permute-start | bytes 49160 | tf_op jit(solution)/shard_map/ppermute | solution.py:22
  42.7 33.3 %collective-permute-start.13 = (bf16[2,2,2048]{2,1,0:T(2,128)(2,1)S(1)}, bf16[2,2,2048]{2,1,0:T(2,128)(2,1)S(1)}, u32[]{:S(2)}, u32[]{:S(2)}) collective-permute-start(bf16[2,2,2048]{2,1,0:T(2,128)(2,1)S(1)} %copy.22), channel_id=1, source_target_pairs={{4,0},{8,4},{12,8},{16,12},{20,16},{24,20},{28,24},{32,28},{36,32}... | collective-permute-start | bytes 49160 | tf_op jit(solution)/shard_map/ppermute | solution.py:25
  72.5 14.4 %collective-permute-start.8 = (bf16[2,2,2048]{2,1,0:T(2,128)(2,1)S(1)}, bf16[2,2,2048]{2,1,0:T(2,128)(2,1)S(1)}, u32[]{:S(2)}, u32[]{:S(2)}) collective-permute-start(bf16[2,2,2048]{2,1,0:T(2,128)(2,1)S(1)} %copy.14), channel_id=1, source_target_pairs={{0,4},{4,8},{8,12},{12,16},{16,20},{20,24},{24,28},{28,32},{32,36}... | collective-permute-start | bytes 49160 | tf_op jit(solution)/shard_map/ppermute | solution.py:22
  74.2 13.2 %collective-permute-start.9 = (bf16[2,2,2048]{2,1,0:T(2,128)(2,1)S(1)}, bf16[2,2,2048]{2,1,0:T(2,128)(2,1)S(1)}, u32[]{:S(2)}, u32[]{:S(2)}) collective-permute-start(bf16[2,2,2048]{2,1,0:T(2,128)(2,1)S(1)} %copy.15), channel_id=1, source_target_pairs={{4,0},{8,4},{12,8},{16,12},{20,16},{24,20},{28,24},{32,28},{36,32}... | collective-permute-start | bytes 49160 | tf_op jit(solution)/shard_map/ppermute | solution.py:25
  81.2 17.7 %collective-permute-start.14 = (bf16[2,132,2]{1,2,0:T(2,128)(2,1)S(1)}, bf16[2,132,2]{1,2,0:T(2,128)(2,1)S(1)}, u32[]{:S(2)}, u32[]{:S(2)}) collective-permute-start(bf16[2,132,2]{1,2,0:T(2,128)(2,1)S(1)} %get-tuple-element.119), channel_id=1, source_target_pairs={{0,1},{1,2},{2,3},{4,5},{5,6},{6,7},{8,9},{9,10},{10,11},{12,13},{... | collective-permute-start | bytes 3176 | tf_op jit(solution)/shard_map/ppermute | solution.py:22
  85.6 13.2 %collective-permute-start.15 = (bf16[2,132,2]{1,2,0:T(2,128)(2,1)S(1)}, bf16[2,132,2]{1,2,0:T(2,128)(2,1)S(1)}, u32[]{:S(2)}, u32[]{:S(2)}) collective-permute-start(bf16[2,132,2]{1,2,0:T(2,128)(2,1)S(1)} %get-tuple-element.118), channel_id=1, source_target_pairs={{1,0},{2,1},{3,2},{5,4},{6,5},{7,6},{9,8},{10,9},{11,10},{13,12},{... | collective-permute-start | bytes 3176 | tf_op jit(solution)/shard_map/ppermute | solution.py:25
  90.5 19.0 %collective-permute-start.10 = (bf16[2,132,2]{1,2,0:T(2,128)(2,1)S(1)}, bf16[2,132,2]{1,2,0:T(2,128)(2,1)S(1)}, u32[]{:S(2)}, u32[]{:S(2)}) collective-permute-start(bf16[2,132,2]{1,2,0:T(2,128)(2,1)S(1)} %get-tuple-element.121), channel_id=1, source_target_pairs={{0,1},{1,2},{2,3},{4,5},{5,6},{6,7},{8,9},{9,10},{10,11},{12,13},{... | collective-permute-start | bytes 3176 | tf_op jit(solution)/shard_map/ppermute | solution.py:22
  96.8 12.7 %collective-permute-start.11 = (bf16[2,132,2]{1,2,0:T(2,128)(2,1)S(1)}, bf16[2,132,2]{1,2,0:T(2,128)(2,1)S(1)}, u32[]{:S(2)}, u32[]{:S(2)}) collective-permute-start(bf16[2,132,2]{1,2,0:T(2,128)(2,1)S(1)} %get-tuple-element.120), channel_id=1, source_target_pairs={{1,0},{2,1},{3,2},{5,4},{6,5},{7,6},{9,8},{10,9},{11,10},{13,12},{... | collective-permute-start | bytes 3176 | tf_op jit(solution)/shard_map/ppermute | solution.py:25
  122.2 3.8 copy-start.1
  126.1 5.3 %collective-permute-start = (f32[2,2,2048]{2,1,0:T(2,128)S(1)}, f32[2,2,2048]{2,1,0:T(2,128)S(1)}, u32[]{:S(2)}, u32[]{:S(2)}) collective-permute-start(f32[2,2,2048]{2,1,0:T(2,128)S(1)} %get-tuple-element.177), channel_id=1, source_target_pairs={{4,0},{8,4},{12,8},{16,12},{20,16},{24,20},{28,24},{32,28},{36,32}... | collective-permute-start | bytes 98312 | tf_op jit(solution)/shard_map/while/body/eval_jaxpr/ppermute | solution.py:25
  127.4 4.8 %collective-permute-start.1 = (f32[2,2,2048]{2,1,0:T(2,128)S(1)}, f32[2,2,2048]{2,1,0:T(2,128)S(1)}, u32[]{:S(2)}, u32[]{:S(2)}) collective-permute-start(f32[2,2,2048]{2,1,0:T(2,128)S(1)} %get-tuple-element.178), channel_id=1, source_target_pairs={{0,4},{4,8},{8,12},{12,16},{16,20},{20,24},{24,28},{28,32},{32,36}... | collective-permute-start | bytes 98312 | tf_op jit(solution)/shard_map/while/body/eval_jaxpr/ppermute | solution.py:22
  134.0 9.0 %collective-permute-start.2 = (f32[2,132,2]{2,1,0:T(8,128)S(1)}, f32[2,132,2]{2,1,0:T(8,128)S(1)}, u32[]{:S(2)}, u32[]{:S(2)}) collective-permute-start(f32[2,132,2]{2,1,0:T(8,128)S(1)} %get-tuple-element.179), channel_id=1, source_target_pairs={{0,1},{1,2},{2,3},{4,5},{5,6},{6,7},{8,9},{9,10},{10,11},{12,13},{... | collective-permute-start | bytes 6344 | tf_op jit(solution)/shard_map/while/body/eval_jaxpr/ppermute | solution.py:22
  140.4 8.9 %collective-permute-start.3 = (f32[2,132,2]{2,1,0:T(8,128)S(1)}, f32[2,132,2]{2,1,0:T(8,128)}, u32[]{:S(2)}, u32[]{:S(2)}) collective-permute-start(f32[2,132,2]{2,1,0:T(8,128)S(1)} %get-tuple-element.180), channel_id=1, source_target_pairs={{1,0},{2,1},{3,2},{5,4},{6,5},{7,6},{9,8},{10,9},{11,10},{13,12},{... | collective-permute-start | bytes 6344 | tf_op jit(solution)/shard_map/while/body/eval_jaxpr/ppermute | solution.py:25
  156.4 5.7 %collective-permute-start = (f32[2,2,2048]{2,1,0:T(2,128)S(1)}, f32[2,2,2048]{2,1,0:T(2,128)S(1)}, u32[]{:S(2)}, u32[]{:S(2)}) collective-permute-start(f32[2,2,2048]{2,1,0:T(2,128)S(1)} %get-tuple-element.177), channel_id=1, source_target_pairs={{4,0},{8,4},{12,8},{16,12},{20,16},{24,20},{28,24},{32,28},{36,32}... | collective-permute-start | bytes 98312 | tf_op jit(solution)/shard_map/while/body/eval_jaxpr/ppermute | solution.py:25
  157.7 5.3 %collective-permute-start.1 = (f32[2,2,2048]{2,1,0:T(2,128)S(1)}, f32[2,2,2048]{2,1,0:T(2,128)S(1)}, u32[]{:S(2)}, u32[]{:S(2)}) collective-permute-start(f32[2,2,2048]{2,1,0:T(2,128)S(1)} %get-tuple-element.178), channel_id=1, source_target_pairs={{0,4},{4,8},{8,12},{12,16},{16,20},{20,24},{24,28},{28,32},{32,36}... | collective-permute-start | bytes 98312 | tf_op jit(solution)/shard_map/while/body/eval_jaxpr/ppermute | solution.py:22
  164.7 8.3 %collective-permute-start.2 = (f32[2,132,2]{2,1,0:T(8,128)S(1)}, f32[2,132,2]{2,1,0:T(8,128)S(1)}, u32[]{:S(2)}, u32[]{:S(2)}) collective-permute-start(f32[2,132,2]{2,1,0:T(8,128)S(1)} %get-tuple-element.179), channel_id=1, source_target_pairs={{0,1},{1,2},{2,3},{4,5},{5,6},{6,7},{8,9},{9,10},{10,11},{12,13},{... | collective-permute-start | bytes 6344 | tf_op jit(solution)/shard_map/while/body/eval_jaxpr/ppermute | solution.py:22
  170.5 8.0 %collective-permute-start.3 = (f32[2,132,2]{2,1,0:T(8,128)S(1)}, f32[2,132,2]{2,1,0:T(8,128)}, u32[]{:S(2)}, u32[]{:S(2)}) collective-permute-start(f32[2,132,2]{2,1,0:T(8,128)S(1)} %get-tuple-element.180), channel_id=1, source_target_pairs={{1,0},{2,1},{3,2},{5,4},{6,5},{7,6},{9,8},{10,9},{11,10},{13,12},{... | collective-permute-start | bytes 6344 | tf_op jit(solution)/shard_map/while/body/eval_jaxpr/ppermute | solution.py:25
  185.5 7.5 %collective-permute-start.4 = (f32[2,2,2048]{2,1,0:T(2,128)S(1)}, f32[2,2,2048]{2,1,0:T(2,128)S(1)}, u32[]{:S(2)}, u32[]{:S(2)}) collective-permute-start(f32[2,2,2048]{2,1,0:T(2,128)S(1)} %get-tuple-element.184), channel_id=1, source_target_pairs={{4,0},{8,4},{12,8},{16,12},{20,16},{24,20},{28,24},{32,28},{36,32}... | collective-permute-start | bytes 98312 | tf_op jit(solution)/shard_map/while/body/eval_jaxpr/ppermute | solution.py:25
  186.8 7.1 %collective-permute-start.5 = (f32[2,2,2048]{2,1,0:T(2,128)S(1)}, f32[2,2,2048]{2,1,0:T(2,128)S(1)}, u32[]{:S(2)}, u32[]{:S(2)}) collective-permute-start(f32[2,2,2048]{2,1,0:T(2,128)S(1)} %get-tuple-element.185), channel_id=1, source_target_pairs={{0,4},{4,8},{8,12},{12,16},{16,20},{20,24},{24,28},{28,32},{32,36}... | collective-permute-start | bytes 98312 | tf_op jit(solution)/shard_map/while/body/eval_jaxpr/ppermute | solution.py:22
  195.6 6.0 %collective-permute-start.6 = (f32[2,132,2]{2,1,0:T(8,128)S(1)}, f32[2,132,2]{2,1,0:T(8,128)S(1)}, u32[]{:S(2)}, u32[]{:S(2)}) collective-permute-start(f32[2,132,2]{2,1,0:T(8,128)S(1)} %get-tuple-element.186), channel_id=1, source_target_pairs={{0,1},{1,2},{2,3},{4,5},{5,6},{6,7},{8,9},{9,10},{10,11},{12,13},{... | collective-permute-start | bytes 6344 | tf_op jit(solution)/shard_map/while/body/eval_jaxpr/ppermute | solution.py:22
  199.1 8.0 %collective-permute-start.7 = (f32[2,132,2]{2,1,0:T(8,128)S(1)}, f32[2,132,2]{2,1,0:T(8,128)}, u32[]{:S(2)}, u32[]{:S(2)}) collective-permute-start(f32[2,132,2]{2,1,0:T(8,128)S(1)} %get-tuple-element.187), channel_id=1, source_target_pairs={{1,0},{2,1},{3,2},{5,4},{6,5},{7,6},{9,8},{10,9},{11,10},{13,12},{... | collective-permute-start | bytes 6344 | tf_op jit(solution)/shard_map/while/body/eval_jaxpr/ppermute | solution.py:25
  213.0 7.1 %collective-permute-start.4 = (f32[2,2,2048]{2,1,0:T(2,128)S(1)}, f32[2,2,2048]{2,1,0:T(2,128)S(1)}, u32[]{:S(2)}, u32[]{:S(2)}) collective-permute-start(f32[2,2,2048]{2,1,0:T(2,128)S(1)} %get-tuple-element.184), channel_id=1, source_target_pairs={{4,0},{8,4},{12,8},{16,12},{20,16},{24,20},{28,24},{32,28},{36,32}... | collective-permute-start | bytes 98312 | tf_op jit(solution)/shard_map/while/body/eval_jaxpr/ppermute | solution.py:25
  214.3 6.6 %collective-permute-start.5 = (f32[2,2,2048]{2,1,0:T(2,128)S(1)}, f32[2,2,2048]{2,1,0:T(2,128)S(1)}, u32[]{:S(2)}, u32[]{:S(2)}) collective-permute-start(f32[2,2,2048]{2,1,0:T(2,128)S(1)} %get-tuple-element.185), channel_id=1, source_target_pairs={{0,4},{4,8},{8,12},{12,16},{16,20},{20,24},{24,28},{28,32},{32,36}... | collective-permute-start | bytes 98312 | tf_op jit(solution)/shard_map/while/body/eval_jaxpr/ppermute | solution.py:22
  222.6 6.0 %collective-permute-start.6 = (f32[2,132,2]{2,1,0:T(8,128)S(1)}, f32[2,132,2]{2,1,0:T(8,128)S(1)}, u32[]{:S(2)}, u32[]{:S(2)}) collective-permute-start(f32[2,132,2]{2,1,0:T(8,128)S(1)} %get-tuple-element.186), channel_id=1, source_target_pairs={{0,1},{1,2},{2,3},{4,5},{5,6},{6,7},{8,9},{9,10},{10,11},{12,13},{... | collective-permute-start | bytes 6344 | tf_op jit(solution)/shard_map/while/body/eval_jaxpr/ppermute | solution.py:22
  226.0 8.0 %collective-permute-start.7 = (f32[2,132,2]{2,1,0:T(8,128)S(1)}, f32[2,132,2]{2,1,0:T(8,128)}, u32[]{:S(2)}, u32[]{:S(2)}) collective-permute-start(f32[2,132,2]{2,1,0:T(8,128)S(1)} %get-tuple-element.187), channel_id=1, source_target_pairs={{1,0},{2,1},{3,2},{5,4},{6,5},{7,6},{9,8},{10,9},{11,10},{13,12},{... | collective-permute-start | bytes 6344 | tf_op jit(solution)/shard_map/while/body/eval_jaxpr/ppermute | solution.py:25
  240.4 54.9 %copy-start = (f32[2,128,2048]{2,1,0:T(8,128)}, f32[2,128,2048]{2,1,0:T(8,128)S(1)}, u32[]{:S(2)}) copy-start(f32[2,128,2048]{2,1,0:T(8,128)S(1)} %get-tuple-element.85) | copy-start | bytes 6291460
  240.4 18.6 %copy-start.11 = (s32[2048]{0:T(1024)S(1)}, s32[2048]{0:T(1024)}, u32[]{:S(2)}) copy-start(s32[2048]{0:T(1024)} %iota_add_fusion) | copy-start | bytes 24580
  295.3 18.3 %copy-start.10 = (s32[128]{0:T(128)S(1)}, s32[128]{0:T(128)}, u32[]{:S(2)}) copy-start(s32[128]{0:T(128)} %iota_add_fusion.2) | copy-start | bytes 1540
  322.9 103.9 %reduce-scatter.5.cloned.1.call-start = ((), (), s32[]{:S(2)}) async-start(), calls=%async_computation.5 | async-start | bytes 163840 | tf_op jit(solution)/shard_map/reduce_scatter | solution.py:99
  (13 other events, 14.4 us)
Sparse Core Ops, SparseCore 0:
  10.1 28.5 all-gather.4
  41.0 26.8 all-gather.2
  323.1 78.2 reduce-scatter.2
  403.7 23.0 reduce-scatter.4
where the time goes:
time: 443 us; the launch traced here: 435 us
  waiting for transfers between devices  183 us (41%)
  matrix products  80.9 us (18%)
  starting transfers between devices  68.6 us (15%)
  local copies, waits for them, and re-layouts  65.1 us (15%)
  other arithmetic  21.9 us (5%)
  between operations  14.5 us (3%)
    reduce_scatter x1, waiting for transfers between devices, on_device(): lax.psum_scatter(partial_far, 'gy', scatter_dimension=1, tiled=True)  78.4 us
    ppermute x12, starting transfers between devices, extended(): lax.ppermute(lax.slice_in_dim(block, block.shape[dim] - width, None, axis...  52.7 us
    all_gather x2, waiting for transfers between devices, on_device(): whole = lax.all_gather(quarter, 'illum', axis=3, tiled=True)  51.1 us
    concatenate x6, local copies, waits for them, and re-layouts, extended(): block = jnp.concatenate([low, block, high], axis=dim)  34.2 us
    reduce_scatter x1, waiting for transfers between devices, on_device(): far = lax.psum_scatter(by_rows, 'gx', scatter_dimension=2, tiled=True)  25.5 us
    ppermute x12, waiting for transfers between devices, extended(): lax.ppermute(lax.slice_in_dim(block, 0, width, axis=dim), axis, backward)  19.9 us
    dot_general x1, matrix products, on_device(): jnp.dot(real, cos_x, precision=high, preferred_element_type=jnp.float32)  18.6 us
    dot_general x1, matrix products, on_device(): jnp.dot(imag, cos_x, precision=high, preferred_element_type=jnp.float32)  18.3 us
  transfers between devices with their start and end apart: 28, of which 16 were waited for; matrix products, arithmetic and copies ran while one was open for 6% of the time, Pallas kernels for 0%

commit v1 on v0

v1 whole, which is shorter than its diff:
```python
import functools
import math

import jax
import jax.numpy as jnp
import ml_dtypes
import numpy as np
from jax import lax
from jax.experimental import pallas as pl
from jax.experimental.pallas import tpu as pltpu
from jax.sharding import PartitionSpec as P

MESH = pl.DeviceIdType.MESH
SUB = 2
DET = 512
RATE = 0.24
PARTS = 1
F32 = jnp.float32
BF16 = jnp.bfloat16


def split(values):
    high = values.astype(ml_dtypes.bfloat16)
    low = (values - high.astype(np.float64)).astype(ml_dtypes.bfloat16)
    return np.stack([high, low])


def tables(det, cy, cx, ny, nx):
    cols = np.arange(cx)
    kappa = np.arange(det // 2) + 0.5
    angle = 2.0 * math.pi * cols[:, None] * kappa[None, :] / nx
    cos, sin = np.cos(angle), np.sin(angle)
    blocks = []
    for m in range(det // 256):
        blocks += [cos[:, 128 * m : 128 * m + 128], sin[:, 128 * m : 128 * m + 128]]
    wave_x = split(np.concatenate(blocks, axis=1))
    shift = math.pi * cols / nx
    turn = np.stack([np.cos(shift), np.sin(shift)]).astype(np.float32)
    turn = np.broadcast_to(turn.reshape(2, cx // 128, 1, 128), (2, cx // 128, 8, 128)).copy()
    ky = np.arange(det) - det // 2
    waves = []
    for tile in range(ny // cy):
        rows = tile * cy + np.arange(cy)
        angle = 2.0 * math.pi * ((ky[:, None] * rows[None, :]) % ny) / ny
        both = np.concatenate([np.cos(angle), np.sin(angle)], axis=1)
        waves.append(split(both / math.sqrt(ny * nx)))
    return wave_x, turn, np.stack(waves)


def lane_ids(rows):
    return lax.broadcasted_iota(jnp.int32, (rows, 128), 1)


def only_if(ok, value, other):
    flags = jnp.full(value.shape, ok.astype(jnp.int32), jnp.int32)
    return jnp.where(flags > 0, value, other)


def pack_edge(tiles, right):
    lane = lane_ids(8)
    out = jnp.zeros((8, 128), F32)
    for t in range(tiles.shape[0] // 8):
        piece = tiles[8 * t : 8 * t + 8]
        shift = (8 * t + (8 if right else 0)) % 128
        if shift:
            piece = pltpu.roll(piece, shift, 1)
        out = jnp.where(lane // 8 == t, piece, out)
    return out


def unpack_edges(left, right, t, fill, left_ok, right_ok):
    lane = lane_ids(8)
    shift_l, shift_r = (120 - 8 * t) % 128, (128 - 8 * t) % 128
    left = pltpu.roll(left, shift_l, 1) if shift_l else left
    right = pltpu.roll(right, shift_r, 1) if shift_r else right
    left = only_if(left_ok, left, fill)
    right = only_if(right_ok, right, fill)
    return jnp.where(lane < 8, right, jnp.where(lane >= 120, left, fill))


def coefficients(label):
    last = label > 6.5
    swing = jnp.where(last, 8.0, label) * (1.0 / (32.0 * RATE)) - 4.0
    loss = label + jnp.maximum(label - 4.0, 0.0) + jnp.where(last, 6.0, 0.0)
    damp = jnp.where(label < -0.5, 0.0, 1.0 - loss * (1.0 / 256.0))
    return swing, damp


def chunks_of(slices, cy, parts):
    if parts == 1:
        return [(s, 0, cy) for s in range(slices)]
    cut = cy // 2 + 16
    return [(s, a, b) for a, b in ((0, cut), (cut, cy)) for s in range(slices)]


def kernel(
    dims, inc, lab, wx_hbm, ey_hbm, turn, exit_ref, far_ref,
    lab_in, stage, out_stage, labs, edge_src, edges, rowbuf, pack_lab, pack_fld, colbuf, corner,
    fld, swing, damp, lhs, wx, ey, gsend, grecv, rhs, fsend, frecv,
    sem_in, sem_out, ag_send, ag_recv, edge_send, edge_recv, row_send, row_recv,
    col_send, col_recv, cl_send, cl_recv, cor_send, cor_recv, g_send, g_recv, f_send, f_recv,
):
    n_il, n_gy, n_gx = dims
    i, j, g = lax.axis_index("illum"), lax.axis_index("gy"), lax.axis_index("gx")
    slices, cy, qx = lab.shape
    cx = inc.shape[2]
    tiles = cx // 128
    per_q = qx // 128
    det = fsend.shape[0]
    parts = PARTS
    size = cy // parts

    def dev(illum=None, gy=None, gx=None):
        return (
            i if illum is None else illum,
            j if gy is None else gy,
            g if gx is None else gx,
        )

    def add(value, step, count):
        return lax.rem(value + (step + count), count)

    def remote(src, dst, send, recv, target):
        return pltpu.make_async_remote_copy(
            src_ref=src, dst_ref=dst, send_sem=send, recv_sem=recv,
            device_id=target, device_id_type=MESH,
        )

    load_lab = pltpu.make_async_copy(lab, lab_in, sem_in.at[0])
    load_fld = pltpu.make_async_copy(inc, stage, sem_in.at[1])
    load_wx = pltpu.make_async_copy(wx_hbm, wx, sem_in.at[2])
    load_ey = pltpu.make_async_copy(ey_hbm.at[j], ey, sem_in.at[3])
    load_lab.start()
    load_fld.start()

    barrier = pltpu.get_barrier_semaphore()
    peers = [dev(illum=add(i, d, n_il)) for d in range(1, n_il)]
    for step in (-1, 1):
        peers += [dev(illum=k, gy=add(j, step, n_gy)) for k in range(n_il)]
        peers += [dev(illum=k, gx=add(g, step, n_gx)) for k in range(n_il)]
    peers += [dev(gx=add(g, d, n_gx)) for d in range(2, n_gx - 1)]
    peers += [dev(gy=add(j, d, n_gy)) for d in range(2, n_gy - 1)]
    for peer in peers:
        pl.semaphore_signal(barrier, inc=1, device_id=peer, device_id_type=MESH)
    load_wx.start()
    load_ey.start()

    load_lab.wait()
    for s in range(slices):
        labs[i, s] = lab_in[s].astype(F32).astype(BF16)
    for e, top in ((0, 0), (1, cy - 8)):
        both = jnp.concatenate([lab_in[s, top : top + 8, :].astype(F32) for s in range(slices)])
        edge_src[e] = both.astype(BF16)
    for s in range(slices):
        pack_lab[0, s] = pack_edge(lab_in[s, :, 0:128].astype(F32), False)
        pack_lab[1, s] = pack_edge(lab_in[s, :, qx - 128 : qx].astype(F32), True)
    load_fld.wait()
    for f in range(2):
        pack_fld[0, f] = pack_edge(stage[f, :, 0:128], False)
        pack_fld[1, f] = pack_edge(stage[f, :, cx - 128 : cx], True)

    pl.semaphore_wait(barrier, len(peers))

    chunks = chunks_of(slices, cy, parts)
    il_next, il_prev = add(i, 1, n_il), add(i, -1, n_il)
    il_far = add(i, 2, n_il)

    def chunk_copy(n, way, second, quarter):
        s, a, b = chunks[n]
        mid = a + (b - a) // 32 * 16
        if second:
            a, b = (a, mid) if way == 0 else (mid, b)
        view = labs.at[quarter, s, pl.ds(a, b - a), :]
        slot = 2 * way + int(second)
        return remote(
            view, view, ag_send.at[n, slot], ag_recv.at[n, slot],
            dev(illum=il_next if way == 0 else il_prev),
        )

    pending = []

    def go(copy):
        copy.start()
        pending.append(copy)

    for way in range(2):
        go(chunk_copy(0, way, False, i))
    col_copies, cl_pairs = [], []
    for side, step in ((0, -1), (1, 1)):
        there = add(g, step, n_gx)
        go(remote(
            pack_fld.at[side], colbuf.at[1 - side, pl.ds(0, 2)], col_send.at[side], col_recv.at[side],
            dev(gx=there),
        ))
        @pl.when(i == (0 if side == 0 else n_il - 1))
        def _():
            for k in range(n_il):
                remote(
                    pack_lab.at[side], colbuf.at[1 - side, pl.ds(2, 2)],
                    cl_send.at[side, k], cl_recv.at[side], dev(illum=k, gx=there),
                ).start()
    for side, step in ((0, -1), (1, 1)):
        there = add(j, step, n_gy)
        src = stage.at[:, pl.ds(0 if side == 0 else cy - 8, 8), :]
        go(remote(src, rowbuf.at[1 - side], row_send.at[side], row_recv.at[side], dev(gy=there)))
        for d in range(n_il):
            go(remote(
                edge_src.at[side], edges.at[1 - side, i], edge_send.at[side, d], edge_recv.at[side, d],
                dev(illum=add(i, d, n_il), gy=there),
            ))
    for n in range(1, len(chunks)):
        for way in range(2):
            go(chunk_copy(n, way, False, i))

    for side in range(2):
        remote(pack_fld.at[side], colbuf.at[1 - side, pl.ds(0, 2)], col_send.at[side], col_recv.at[side], dev()).wait_recv()
        remote(pack_lab.at[side], colbuf.at[1 - side, pl.ds(2, 2)], cl_send.at[side, 0], cl_recv.at[side], dev()).wait_recv()
    for side, step in ((0, -1), (1, 1)):
        go(remote(
            colbuf, corner.at[1 - side], cor_send.at[side], cor_recv.at[side],
            dev(gy=add(j, step, n_gy)),
        ))

    def forward(n):
        for way in range(2):
            src = il_prev if way == 0 else il_next
            chunk_copy(n, way, False, src).wait_recv()
            go(chunk_copy(n, way, True, src))

    def arrived(n):
        for way in range(2):
            chunk_copy(n, way, True, il_far).wait_recv()

    up_ok, down_ok = j > 0, j < n_gy - 1
    left_ok, right_ok = g > 0, g < n_gx - 1

    def assemble_field(h):
        first = h * size
        for f in range(2):
            def main(c, carry):
                lanes = pl.ds(pl.multiple_of(c * 128, 128), 128)
                fld[f, c, 0:8, :] = jnp.zeros((8, 128), F32)
                fld[f, c, size + 24 : size + 32, :] = jnp.zeros((8, 128), F32)
                fld[f, c, 16 : size + 16, :] = stage[f, first : first + size, lanes]
                if h == 0:
                    fld[f, c, 8:16, :] = only_if(up_ok, rowbuf[0, f, :, lanes], 0.0)
                else:
                    fld[f, c, 8:16, :] = stage[f, first - 8 : first, lanes]
                if h == parts - 1:
                    fld[f, c, size + 16 : size + 24, :] = only_if(down_ok, rowbuf[1, f, :, lanes], 0.0)
                else:
                    fld[f, c, size + 16 : size + 24, :] = stage[f, first + size : first + size + 8, lanes]
                return carry

            lax.fori_loop(0, tiles, main, 0)
            fld[f, tiles, 0:8, :] = jnp.zeros((8, 128), F32)
            fld[f, tiles, size + 24 : size + 32, :] = jnp.zeros((8, 128), F32)

        def put(f, row, value):
            fld[f, tiles, row : row + 8, :] = value

        edge_tiles(h, (0, 1), 0.0, put)

    def edge_tiles(h, which, fill, put):
        total = cy // 8
        for w in which:
            left, right = colbuf[0, w], colbuf[1, w]
            for t in range(h * size // 8 - 1, (h + 1) * size // 8 + 1):
                row = 16 + 8 * t - h * size
                if t < 0:
                    value = unpack_edges(corner[0, 0, w], corner[0, 1, w], total - 1, fill, left_ok & up_ok, right_ok & up_ok)
                elif t >= total:
                    value = unpack_edges(corner[1, 0, w], corner[1, 1, w], 0, fill, left_ok & down_ok, right_ok & down_ok)
                else:
                    value = unpack_edges(left, right, t, fill, left_ok, right_ok)
                put(w, row, value)

    def set_coefs(c, row, rows, label):
        a, b = coefficients(label)
        swing[c, row : row + rows, :] = a
        damp[c, row : row + rows, :] = b

    def assemble_coefs(h, s):
        first = h * size

        def main(c, carry):
            q = c // per_q
            lanes = pl.ds(pl.multiple_of(lax.rem(c, per_q) * 128, 128), 128)
            set_coefs(c, 16, size, labs[q, s, first : first + size, lanes].astype(F32))
            if h == 0:
                top = only_if(up_ok, edges[0, q, :, lanes].astype(F32)[8 * s : 8 * s + 8], -1.0)
            else:
                top = labs[q, s, first - 16 : first, lanes].astype(F32)[8:16]
            set_coefs(c, 8, 8, top)
            if h == parts - 1:
                bottom = only_if(down_ok, edges[1, q, :, lanes].astype(F32)[8 * s : 8 * s + 8], -1.0)
            else:
                bottom = labs[q, s, first + size : first + size + 16, lanes].astype(F32)[0:8]
            set_coefs(c, size + 16, 8, bottom)
            return carry

        lax.fori_loop(0, tiles, main, 0)
        edge_tiles(h, (2 + s,), -1.0, lambda w, row, value: set_coefs(tiles, row, 8, value))

    def half_step(target, source, sign):
        lane = lane_ids(8)

        def column(c, carry):
            before = lax.rem(c + tiles, tiles + 1)
            after = lax.rem(c + 1, tiles + 1)
            for t in range(1, size // 8 + 3):
                r = 8 * t
                mid = fld[source, c, r : r + 8, :]
                vert = fld[source, c, r - 1 : r + 7, :] + fld[source, c, r + 1 : r + 9, :]
                left = pltpu.roll(jnp.where(lane == 127, fld[source, before, r : r + 8, :], mid), 1, 1)
                right = pltpu.roll(jnp.where(lane == 0, fld[source, after, r : r + 8, :], mid), 127, 1)
                total = vert + (left + right) + swing[c, r : r + 8, :] * mid
                fld[target, c, r : r + 8, :] = damp[c, r : r + 8, :] * (fld[target, c, r : r + 8, :] + (sign * RATE) * total)
            return carry

        lax.fori_loop(0, tiles + 1, column, 0)

    def transform(h):
        first = h * size

        def modulate(c, carry):
            lanes = pl.ds(pl.multiple_of(c * 128, 128), 128)
            cos = jnp.concatenate([turn[0, c]] * (size // 8))
            sin = jnp.concatenate([turn[1, c]] * (size // 8))
            real = fld[0, c, 16 : size + 16, :]
            imag = fld[1, c, 16 : size + 16, :]
            out_stage[0, first : first + size, lanes] = real
            out_stage[1, first : first + size, lanes] = imag
            for n, value in enumerate((real * cos - imag * sin, real * sin + imag * cos)):
                high = value.astype(BF16)
                lhs[0, n * size : (n + 1) * size, lanes] = high
                lhs[1, n * size : (n + 1) * size, lanes] = (value - high.astype(F32)).astype(BF16)
            return carry

        lax.fori_loop(0, tiles, modulate, 0)
        pltpu.make_async_copy(
            out_stage.at[:, pl.ds(first, size), :], exit_ref.at[:, pl.ds(first, size), :], sem_out.at[h]
        ).start()
        lane = lane_ids(8)
        for m in range(det // 256):
            cols = slice(256 * m, 256 * m + 256)
            prod = jnp.dot(lhs[0], wx[0, :, cols], preferred_element_type=F32)
            prod += jnp.dot(lhs[1], wx[0, :, cols], preferred_element_type=F32)
            prod += jnp.dot(lhs[0], wx[1, :, cols], preferred_element_type=F32)
            c_re, s_re = prod[:size, :128], prod[:size, 128:]
            c_im, s_im = prod[size:, :128], prod[size:, 128:]
            rank = 128 * m + lane
            for block, freq, g_re, g_im in (
                (n_gx // 2 + m, rank, c_re + s_im, c_im - s_re),
                (n_gx // 2 - 1 - m, -rank - 1, c_re - s_im, c_im + s_re),
            ):
                quarter = lax.rem((freq + det) * g, n_gx) * (4 // n_gx)
                f_re = jnp.where(quarter == 0, 1.0, jnp.where(quarter == 2, -1.0, 0.0))
                f_im = jnp.where(quarter == 1, -1.0, jnp.where(quarter == 3, 1.0, 0.0))
                f_re = jnp.concatenate([f_re] * (size // 8))
                f_im = jnp.concatenate([f_im] * (size // 8))
                gsend[block, first : first + size, 0:128] = g_re * f_re - g_im * f_im
                gsend[block, first : first + size, 128:256] = g_re * f_im + g_im * f_re

    def g_copy(h, d):
        rows = pl.ds(h * size, size)
        block = add(g, d, n_gx)
        return remote(
            gsend.at[block, rows, :], grecv.at[d - 1, rows, :],
            g_send.at[h, d - 1], g_recv.at[h, d - 1], dev(gx=block),
        )

    per_part = slices
    ready_rows = False
    for h in range(parts):
        for s in range(slices):
            n = h * per_part + s
            forward(n)
            if not ready_rows:
                for side in range(2):
                    remote(stage.at[:, pl.ds(0, 8), :], rowbuf.at[1 - side], row_send.at[side], row_recv.at[side], dev()).wait_recv()
                    for d in range(n_il):
                        remote(edge_src.at[side], edges.at[1 - side, i], edge_send.at[side, d], edge_recv.at[side, d], dev()).wait_recv()
                    remote(colbuf, corner.at[1 - side], cor_send.at[side], cor_recv.at[side], dev()).wait_recv()
                ready_rows = True
            if s == 0:
                assemble_field(h)
            arrived(n)
            assemble_coefs(h, s)

            def substep(step, carry):
                half_step(0, 1, -1.0)
                half_step(1, 0, 1.0)
                return carry

            lax.fori_loop(0, SUB, substep, 0)
        if h == 0:
            load_wx.wait()
        transform(h)
        for d in range(1, n_gx):
            go(g_copy(h, d))

    load_ey.wait()
    for h in range(parts):
        for d in range(1, n_gx):
            g_copy(h, d).wait_recv()
    total = gsend[g]
    for d in range(1, n_gx):
        total = total + grecv[d - 1]
    high = total.astype(BF16)
    low = (total - high.astype(F32)).astype(BF16)
    for n, value in enumerate((high, low)):
        rhs[n, 0:cy, :] = value
        rhs[n, cy : 2 * cy, 0:128] = value[:, 128:256]
        rhs[n, cy : 2 * cy, 128:256] = -value[:, 0:128]
    fsend[...] = (
        jnp.dot(ey[0], rhs[0], preferred_element_type=F32)
        + jnp.dot(ey[1], rhs[0], preferred_element_type=F32)
        + jnp.dot(ey[0], rhs[1], preferred_element_type=F32)
    )
    share = det // n_gy

    def f_copy(d):
        there = add(j, d, n_gy)
        return remote(
            fsend.at[pl.ds(pl.multiple_of(there * share, share), share), :], frecv.at[d - 1],
            f_send.at[d - 1], f_recv.at[d - 1], dev(gy=there),
        )

    for d in range(1, n_gy):
        go(f_copy(d))
    acc = fsend[pl.ds(pl.multiple_of(j * share, share), share), :]
    for d in range(1, n_gy):
        f_copy(d).wait_recv()
        acc = acc + frecv[d - 1]
    row_id = lax.broadcasted_iota(jnp.int32, (128, 128), 0)
    col_id = lax.broadcasted_iota(jnp.int32, (128, 128), 1)
    mirror = jnp.full((128, 128), (g < n_gx // 2).astype(jnp.int32), jnp.int32)
    order = jnp.where(jnp.where(mirror > 0, 127 - col_id, col_id) == row_id, 1.0, 0.0)
    for n in range(2):
        far_ref[n] = jnp.dot(
            acc[:, 128 * n : 128 * n + 128], order, precision=lax.Precision.HIGHEST, preferred_element_type=F32
        )

    for copy in pending:
        copy.wait_send()
    for side in range(2):
        @pl.when(i == (0 if side == 0 else n_il - 1))
        def _():
            for k in range(n_il):
                remote(pack_lab.at[side], colbuf.at[1 - side, pl.ds(2, 2)], cl_send.at[side, k], cl_recv.at[side], dev()).wait_send()
    for h in range(parts):
        rows = pl.ds(h * size, size)
        pltpu.make_async_copy(out_stage.at[:, rows, :], exit_ref.at[:, rows, :], sem_out.at[h]).wait()


def on_device(dims, det, incident, labels):
    n_il, n_gy, n_gx = dims
    slices, cy = labels.shape[:2]
    qx = labels.shape[4]
    cx = incident.shape[3]
    ny, nx = cy * n_gy, cx * n_gx
    wave_x, turn, wave_y = tables(det, cy, cx, ny, nx)
    tiles = cx // 128
    size = cy // PARTS
    share = det // n_gy
    n_chunks = len(chunks_of(slices, cy, PARTS))
    dma = pltpu.SemaphoreType.DMA
    vmem = pltpu.VMEM
    any_spec = pl.BlockSpec(memory_space=pl.ANY)
    vmem_spec = pl.BlockSpec(memory_space=pltpu.VMEM)
    field, far = pl.pallas_call(
        functools.partial(kernel, dims),
        out_shape=(
            jax.ShapeDtypeStruct((2, cy, cx), F32),
            jax.ShapeDtypeStruct((2, share, 128), F32),
        ),
        in_specs=[any_spec] * 4 + [vmem_spec],
        out_specs=(any_spec, vmem_spec),
        scratch_shapes=[
            vmem((slices, cy, qx), jnp.int32),
            vmem((2, cy, cx), F32),
            vmem((2, cy, cx), F32),
            vmem((n_il, slices, cy, qx), BF16),
            vmem((2, 8 * slices, qx), BF16),
            vmem((2, n_il, 8 * slices, qx), BF16),
            vmem((2, 2, 8, cx), F32),
            vmem((2, slices, 8, 128), F32),
            vmem((2, 2, 8, 128), F32),
            vmem((2, 2 + slices, 8, 128), F32),
            vmem((2, 2, 2 + slices, 8, 128), F32),
            vmem((2, tiles + 1, size + 32, 128), F32),
            vmem((tiles + 1, size + 32, 128), F32),
            vmem((tiles + 1, size + 32, 128), F32),
            vmem((2, 2 * size, cx), BF16),
            vmem((2, cx, det), BF16),
            vmem((2, det, 2 * cy), BF16),
            vmem((n_gx, cy, 256), F32),
            vmem((n_gx - 1, cy, 256), F32),
            vmem((2, 2 * cy, 256), BF16),
            vmem((det, 256), F32),
            vmem((n_gy - 1, share, 256), F32),
            dma((4,)),
            dma((PARTS,)),
            dma((n_chunks, 4)),
            dma((n_chunks, 4)),
            dma((2, n_il)),
            dma((2, n_il)),
            dma((2,)),
            dma((2,)),
            dma((2,)),
            dma((2,)),
            dma((2, n_il)),
            dma((2,)),
            dma((2,)),
            dma((2,)),
            dma((PARTS, n_gx - 1)),
            dma((PARTS, n_gx - 1)),
            dma((n_gy - 1,)),
            dma((n_gy - 1,)),
        ],
        compiler_params=pltpu.CompilerParams(
            collective_id=0, has_side_effects=True, vmem_limit_bytes=48 * 1024 * 1024
        ),
    )(
        incident.reshape(2, cy, cx),
        labels.reshape(slices, cy, qx),
        jnp.asarray(wave_x),
        jnp.asarray(wave_y),
        jnp.asarray(turn),
    )
    return field[None], far[None]


def solution(mesh, det=DET):
    dims = tuple(mesh.shape[name] for name in ("illum", "gy", "gx"))
    in_specs = (P("illum", None, "gy", "gx"), P(None, "gy", "gx", "illum", None))
    out_specs = (P("illum", None, "gy", "gx"), P("illum", None, "gy", "gx"))
    return jax.shard_map(
        functools.partial(on_device, dims, det), mesh=mesh, in_specs=in_specs, out_specs=out_specs, check_vma=False
    )
```

time: 443 us -> 244 us (0.55)
  the two profiles are of different devices: /device:TPU:2 before, /device:TPU:1 now
where the time goes in v1:
time: 244 us
  Pallas kernels  238 us (98%)
  local copies, waits for them, and re-layouts  5.5 us (2%)
    pallas_call x1, Pallas kernels, on_device(): pl.pallas_call(functools.partial(kernel, dims), out_shape=(jax.ShapeDtype...  238 us
    unnamed x7, local copies, waits for them, and re-layouts  5.5 us

profile of v1, /device:TPU:1, one launch (start us, length us, event | category | flops | bytes accessed | tf_op | source)
XLA Modules:
  0.0 244.2 jit_solution(11646616086361034815)
XLA Ops:
  0.6 1.1 copy.9
  1.7 0.0 copy-start
  1.7 1.6 copy-done
  3.3 0.0 copy-start.1
  3.3 0.9 copy-done.1
  4.2 238.1 %shard_map.68 = (f32[2,128,2048]{2,1,0:T(8,128)S(1)}, f32[2,32,128]{2,1,0:T(8,128)S(1)}) custom-call(f32[2,128,2048]{2,1,0:T(8,128)S(1)} %bitcast.7, s32[2,128,512]{2,1,0:T(8,128)S(1)} %bitcast.8, bf16[2,2048,512]{2,1,0:T(8,128)(2,1)} %constant.6.clone.wx_hbm, bf16[16,2,512,256]{3,2,1,0:T(8,128)(2,1)} %constant.7.clone.ey_hbm, f32[2,16,8,128]{3,2,1,0:T(8,128)S(1)} %copy-done.1), custom_call_target="tpu_custom_call" | custom-call | tf_op jit(solution)/shard_map/pallas_call | solution.py:472
  242.3 1.3 copy.12
  243.6 0.6 copy.13
Async XLA Ops:
  1.7 1.6 copy-start
  3.3 0.9 copy-start.1

commit v2 on v1

--- a/solution.py
+++ b/solution.py
@@ -96,11 +96,12 @@
 def kernel(
     dims, inc, lab, wx_hbm, ey_hbm, turn, exit_ref, far_ref,
     lab_in, stage, out_stage, labs, edge_src, edges, rowbuf, pack_lab, pack_fld, colbuf, corner,
-    fld, swing, damp, lhs, wx, ey, gsend, grecv, rhs, fsend, frecv,
+    fld_re, fld_im, swing, damp, lhs, wx, ey, gsend, grecv, rhs, fsend, frecv,
     sem_in, sem_out, ag_send, ag_recv, edge_send, edge_recv, row_send, row_recv,
     col_send, col_recv, cl_send, cl_recv, cor_send, cor_recv, g_send, g_recv, f_send, f_recv,
 ):
     n_il, n_gy, n_gx = dims
+    fld = (fld_re, fld_im)
     i, j, g = lax.axis_index("illum"), lax.axis_index("gy"), lax.axis_index("gx")
     slices, cy, qx = lab.shape
     cx = inc.shape[2]
@@ -239,25 +240,25 @@
         for f in range(2):
             def main(c, carry):
                 lanes = pl.ds(pl.multiple_of(c * 128, 128), 128)
-                fld[f, c, 0:8, :] = jnp.zeros((8, 128), F32)
-                fld[f, c, size + 24 : size + 32, :] = jnp.zeros((8, 128), F32)
-                fld[f, c, 16 : size + 16, :] = stage[f, first : first + size, lanes]
+                fld[f][c, 0:8, :] = jnp.zeros((8, 128), F32)
+                fld[f][c, size + 24 : size + 32, :] = jnp.zeros((8, 128), F32)
+                fld[f][c, 16 : size + 16, :] = stage[f, first : first + size, lanes]
                 if h == 0:
-                    fld[f, c, 8:16, :] = only_if(up_ok, rowbuf[0, f, :, lanes], 0.0)
+                    fld[f][c, 8:16, :] = only_if(up_ok, rowbuf[0, f, :, lanes], 0.0)
                 else:
-                    fld[f, c, 8:16, :] = stage[f, first - 8 : first, lanes]
+                    fld[f][c, 8:16, :] = stage[f, first - 8 : first, lanes]
                 if h == parts - 1:
-                    fld[f, c, size + 16 : size + 24, :] = only_if(down_ok, rowbuf[1, f, :, lanes], 0.0)
+                    fld[f][c, size + 16 : size + 24, :] = only_if(down_ok, rowbuf[1, f, :, lanes], 0.0)
                 else:
-                    fld[f, c, size + 16 : size + 24, :] = stage[f, first + size : first + size + 8, lanes]
+                    fld[f][c, size + 16 : size + 24, :] = stage[f, first + size : first + size + 8, lanes]
                 return carry
 
             lax.fori_loop(0, tiles, main, 0)
-            fld[f, tiles, 0:8, :] = jnp.zeros((8, 128), F32)
-            fld[f, tiles, size + 24 : size + 32, :] = jnp.zeros((8, 128), F32)
+            fld[f][tiles, 0:8, :] = jnp.zeros((8, 128), F32)
+            fld[f][tiles, size + 24 : size + 32, :] = jnp.zeros((8, 128), F32)
 
         def put(f, row, value):
-            fld[f, tiles, row : row + 8, :] = value
+            fld[f][tiles, row : row + 8, :] = value
 
         edge_tiles(h, (0, 1), 0.0, put)
 
@@ -303,22 +304,21 @@
         edge_tiles(h, (2 + s,), -1.0, lambda w, row, value: set_coefs(tiles, row, 8, value))
 
     def half_step(target, source, sign):
-        lane = lane_ids(8)
-
-        def column(c, carry):
-            before = lax.rem(c + tiles, tiles + 1)
-            after = lax.rem(c + 1, tiles + 1)
-            for t in range(1, size // 8 + 3):
-                r = 8 * t
-                mid = fld[source, c, r : r + 8, :]
-                vert = fld[source, c, r - 1 : r + 7, :] + fld[source, c, r + 1 : r + 9, :]
-                left = pltpu.roll(jnp.where(lane == 127, fld[source, before, r : r + 8, :], mid), 1, 1)
-                right = pltpu.roll(jnp.where(lane == 0, fld[source, after, r : r + 8, :], mid), 127, 1)
-                total = vert + (left + right) + swing[c, r : r + 8, :] * mid
-                fld[target, c, r : r + 8, :] = damp[c, r : r + 8, :] * (fld[target, c, r : r + 8, :] + (sign * RATE) * total)
-            return carry
-
-        lax.fori_loop(0, tiles + 1, column, 0)
+        rows = size + 16
+        lane = lane_ids(rows)
+
+        def column(c):
+            before = (c + tiles) % (tiles + 1)
+            after = (c + 1) % (tiles + 1)
+            mid = source[c, 8 : 8 + rows, :]
+            vert = source[c, 7 : 7 + rows, :] + source[c, 9 : 9 + rows, :]
+            left = pltpu.roll(jnp.where(lane == 127, source[before, 8 : 8 + rows, :], mid), 1, 1)
+            right = pltpu.roll(jnp.where(lane == 0, source[after, 8 : 8 + rows, :], mid), 127, 1)
+            total = vert + (left + right) + swing[c, 8 : 8 + rows, :] * mid
+            target[c, 8 : 8 + rows, :] = damp[c, 8 : 8 + rows, :] * (target[c, 8 : 8 + rows, :] + (sign * RATE) * total)
+
+        for c in range(tiles + 1):
+            column(c)
 
     def transform(h):
         first = h * size
@@ -327,8 +327,8 @@
             lanes = pl.ds(pl.multiple_of(c * 128, 128), 128)
             cos = jnp.concatenate([turn[0, c]] * (size // 8))
             sin = jnp.concatenate([turn[1, c]] * (size // 8))
-            real = fld[0, c, 16 : size + 16, :]
-            imag = fld[1, c, 16 : size + 16, :]
+            real = fld[0][c, 16 : size + 16, :]
+            imag = fld[1][c, 16 : size + 16, :]
             out_stage[0, first : first + size, lanes] = real
             out_stage[1, first : first + size, lanes] = imag
             for n, value in enumerate((real * cos - imag * sin, real * sin + imag * cos)):
@@ -389,8 +389,8 @@
             assemble_coefs(h, s)
 
             def substep(step, carry):
-                half_step(0, 1, -1.0)
-                half_step(1, 0, 1.0)
+                half_step(fld[0], fld[1], -1.0)
+                half_step(fld[1], fld[0], 1.0)
                 return carry
 
             lax.fori_loop(0, SUB, substep, 0)
@@ -489,7 +489,8 @@
             vmem((2, 2, 8, 128), F32),
             vmem((2, 2 + slices, 8, 128), F32),
             vmem((2, 2, 2 + slices, 8, 128), F32),
-            vmem((2, tiles + 1, size + 32, 128), F32),
+            vmem((tiles + 1, size + 32, 128), F32),
+            vmem((tiles + 1, size + 32, 128), F32),
             vmem((tiles + 1, size + 32, 128), F32),
             vmem((tiles + 1, size + 32, 128), F32),
             vmem((2, 2 * size, cx), BF16),

time: 244 us -> 63.3 us (0.26)
  Pallas kernels: 238 us -> 57 us
    pallas_call x1, Pallas kernels: 238 us -> 57 us  [on_device(): pl.pallas_call(functools.partial(kernel, dims), out_shape=(jax.ShapeDtype...]
where the time goes in v2:
time: 63.3 us; the launch traced here: 63.1 us
  Pallas kernels  57 us (90%)
  local copies, waits for them, and re-layouts  5.5 us (9%)
  between operations  0.65 us (1%)
    pallas_call x1, Pallas kernels, on_device(): pl.pallas_call(functools.partial(kernel, dims), out_shape=(jax.ShapeDtype...  57 us
    unnamed x7, local copies, waits for them, and re-layouts  5.5 us

profile of v2, /device:TPU:1, one launch (start us, length us, event | category | flops | bytes accessed | tf_op | source)
XLA Modules:
  0.0 63.1 jit_solution(6428899133834399372)
XLA Ops:
  0.6 1.1 %copy.9 = s32[2,128,1,1,512]{4,1,2,3,0:T(8,128)S(1)} copy(s32[2,128,1,1,512]{4,3,2,1,0:T(1,128)} %param.6) | data formatting | bytes 1048576
  1.7 0.0 copy-start
  1.7 1.6 %copy-done = f32[1,2,128,2048]{3,2,1,0:T(8,128)S(1)} copy-done((f32[1,2,128,2048]{3,2,1,0:T(8,128)S(1)}, f32[1,2,128,2048]{3,2,1,0:T(8,128)}, u32[]{:S(2)}) %copy-start) | copy-done | bytes 2097176
  3.3 0.0 copy-start.1
  3.3 0.9 %copy-done.1 = f32[2,16,8,128]{3,2,1,0:T(8,128)S(1)} copy-done((f32[2,16,8,128]{3,2,1,0:T(8,128)S(1)}, f32[2,16,8,128]{3,2,1,0:T(8,128)}, u32[]{:S(2)}) %copy-start.1) | copy-done | bytes 131096
  4.2 57.0 %shard_map.68 = (f32[2,128,2048]{2,1,0:T(8,128)S(1)}, f32[2,32,128]{2,1,0:T(8,128)S(1)}) custom-call(f32[2,128,2048]{2,1,0:T(8,128)S(1)} %bitcast.7, s32[2,128,512]{2,1,0:T(8,128)S(1)} %bitcast.8, bf16[2,2048,512]{2,1,0:T(8,128)(2,1)} %constant.6.clone.wx_hbm, bf16[16,2,512,256]{3,2,1,0:T(8,128)(2,1)} %constant.7.clone.ey_hbm, f32[2,16,8,128]{3,2,1,0:T(8,128)S(1)} %copy-done.1), custom_call_target="tpu_custom_call" | custom-call | tf_op jit(solution)/shard_map/pallas_call | solution.py:472
  61.2 1.3 %copy.12 = f32[1,2,128,2048]{3,2,1,0:T(8,128)} copy(f32[1,2,128,2048]{3,2,1,0:T(8,128)S(1)} %bitcast.6) | data formatting | bytes 4194304
  62.5 0.6 copy.13
Async XLA Ops:
  1.7 1.6 %copy-start = (f32[1,2,128,2048]{3,2,1,0:T(8,128)S(1)}, f32[1,2,128,2048]{3,2,1,0:T(8,128)}, u32[]{:S(2)}) copy-start(f32[1,2,128,2048]{3,2,1,0:T(8,128)} %param.5) | copy-start | bytes 6291460
  3.3 0.9 %copy-start.1 = (f32[2,16,8,128]{3,2,1,0:T(8,128)S(1)}, f32[2,16,8,128]{3,2,1,0:T(8,128)}, u32[]{:S(2)}) copy-start(f32[2,16,8,128]{3,2,1,0:T(8,128)} %constant.8.clone.turn) | copy-start | bytes 393220

commit v3 on v2

v3 whole, which is shorter than its diff:
```python
import functools
import math

import jax
import jax.numpy as jnp
import ml_dtypes
import numpy as np
from jax import lax
from jax.experimental import pallas as pl
from jax.experimental.pallas import tpu as pltpu
from jax.sharding import PartitionSpec as P

MESH = pl.DeviceIdType.MESH
SUB = 2
DET = 512
RATE = 0.24
PARTS = 1
F32 = jnp.float32
BF16 = jnp.bfloat16


def split(values):
    high = values.astype(ml_dtypes.bfloat16)
    low = (values - high.astype(np.float64)).astype(ml_dtypes.bfloat16)
    return np.stack([high, low])


def tables(det, cy, cx, ny, nx):
    cols = np.arange(cx)
    kappa = np.arange(det // 2) + 0.5
    angle = 2.0 * math.pi * cols[:, None] * kappa[None, :] / nx
    cos, sin = np.cos(angle), np.sin(angle)
    blocks = []
    for m in range(det // 256):
        blocks += [cos[:, 128 * m : 128 * m + 128], sin[:, 128 * m : 128 * m + 128]]
    wave_x = split(np.concatenate(blocks, axis=1))
    shift = math.pi * cols / nx
    turn = np.stack([np.cos(shift), np.sin(shift)]).astype(np.float32)
    turn = np.broadcast_to(turn.reshape(2, cx // 128, 1, 128), (2, cx // 128, 8, 128)).copy()
    share = det // (ny // cy)
    ky = (np.arange(det) - det // 2).reshape(-1, 2, share).transpose(1, 0, 2).reshape(-1)
    waves = []
    for tile in range(ny // cy):
        rows = tile * cy + np.arange(cy)
        angle = 2.0 * math.pi * ((ky[:, None] * rows[None, :]) % ny) / ny
        both = np.concatenate([np.cos(angle), np.sin(angle)], axis=1)
        waves.append(split(both / math.sqrt(ny * nx)))
    return wave_x, turn, np.stack(waves)


def lane_ids(rows):
    return lax.broadcasted_iota(jnp.int32, (rows, 128), 1)


def only_if(ok, value, other):
    flags = jnp.full(value.shape, ok.astype(jnp.int32), jnp.int32)
    return jnp.where(flags > 0, value, other)


def pack_edge(tiles, right):
    lane = lane_ids(8)
    out = jnp.zeros((8, 128), F32)
    for t in range(tiles.shape[0] // 8):
        piece = tiles[8 * t : 8 * t + 8]
        shift = (8 * t + (8 if right else 0)) % 128
        if shift:
            piece = pltpu.roll(piece, shift, 1)
        out = jnp.where(lane // 8 == t, piece, out)
    return out


def unpack_edges(left, right, t, fill, left_ok, right_ok):
    lane = lane_ids(8)
    shift_l, shift_r = (120 - 8 * t) % 128, (128 - 8 * t) % 128
    left = pltpu.roll(left, shift_l, 1) if shift_l else left
    right = pltpu.roll(right, shift_r, 1) if shift_r else right
    left = only_if(left_ok, left, fill)
    right = only_if(right_ok, right, fill)
    return jnp.where(lane < 8, right, jnp.where(lane >= 120, left, fill))


def coefficients(label):
    last = label > 6.5
    swing = jnp.where(last, 8.0, label) * (1.0 / (32.0 * RATE)) - 4.0
    loss = label + jnp.maximum(label - 4.0, 0.0) + jnp.where(last, 6.0, 0.0)
    damp = jnp.where(label < -0.5, 0.0, 1.0 - loss * (1.0 / 256.0))
    return swing, damp


def chunks_of(slices, cy, parts):
    if parts == 1:
        return [(s, 0, cy) for s in range(slices)]
    cut = cy // 2 + 16
    return [(s, a, b) for a, b in ((0, cut), (cut, cy)) for s in range(slices)]


def middle(n, a, b):
    step = (b - a) // 32 * 16
    return b - step if n % 2 else a + step


def kernel(
    dims, inc, lab, wx_hbm, ey_hbm, turn_hbm, exit_ref, far_ref,
    lab_in, stage, out_stage, labs, edge_src, pack_lab, ext, rowbuf, pack_fld, colbuf,
    fld_re, fld_im, swing, damp, turn, lhs, wx, ey, gown, gsend, grecv, rhs, fsend, fpair, fhalf, frecv,
    sem_lab, sem_in, sem_out, ag_send, ag_recv, edge_send, edge_recv, cl_send, cl_recv, ext_send, ext_recv,
    row_send, row_recv, col_send, col_recv, g_send, g_recv, pair_sem, f_send, f_recv,
):
    n_il, n_gy, n_gx = dims
    fld = (fld_re, fld_im)
    i, j, g = lax.axis_index("illum"), lax.axis_index("gy"), lax.axis_index("gx")
    _, slices, cy, qx = labs.shape
    cx = inc.shape[2]
    tiles = cx // 128
    per_q = qx // 128
    det = wx.shape[2]
    parts = PARTS
    size = cy // parts

    def dev(illum=None, gy=None, gx=None):
        return (
            i if illum is None else illum,
            j if gy is None else gy,
            g if gx is None else gx,
        )

    def add(value, step, count):
        return lax.rem(value + (step + count), count)

    def remote(src, dst, send, recv, target):
        return pltpu.make_async_remote_copy(
            src_ref=src, dst_ref=dst, send_sem=send, recv_sem=recv,
            device_id=target, device_id_type=MESH,
        )

    lab_rows = cy * per_q
    load_lab = [
        pltpu.make_async_copy(
            lab.at[pl.ds(s * lab_rows, lab_rows), :], lab_in.at[pl.ds(s * lab_rows, lab_rows), :], sem_lab.at[s]
        )
        for s in range(slices)
    ]
    load_fld = pltpu.make_async_copy(inc, stage, sem_in.at[1])
    load_wx = pltpu.make_async_copy(wx_hbm, wx, sem_in.at[2])
    load_ey = pltpu.make_async_copy(ey_hbm.at[j], ey, sem_in.at[3])
    load_turn = pltpu.make_async_copy(turn_hbm, turn, sem_in.at[4])
    for load in load_lab:
        load.start()
    load_fld.start()
    ext[i, 32:48, :] = jnp.zeros((16, qx), BF16)

    barrier = pltpu.get_barrier_semaphore()
    peers = [dev(illum=add(i, d, n_il)) for d in range(1, n_il)]
    peers += [
        dev(gy=add(j, dj, n_gy), gx=add(g, dg, n_gx))
        for dj in (-1, 0, 1) for dg in (-1, 0, 1) if dj or dg
    ]
    peers += [dev(gx=add(g, d, n_gx)) for d in range(2, n_gx - 1)]
    peers += [dev(gy=add(j, d, n_gy)) for d in range(2, n_gy, 2)]
    for peer in peers:
        pl.semaphore_signal(barrier, inc=1, device_id=peer, device_id_type=MESH)
    load_turn.start()
    load_wx.start()
    load_ey.start()

    def label_tile(s, row, rows, tile):
        return lab_in[pl.ds((s * cy + row) * per_q + tile, rows, stride=per_q), :].astype(F32)

    def own_labels(s):
        load_lab[s].wait()
        for tile in range(per_q):
            labs[i, s, :, 128 * tile : 128 * tile + 128] = label_tile(s, 0, cy, tile).astype(BF16)

    def label_edges():
        for e, top in ((0, 0), (1, cy - 8)):
            for tile in range(per_q):
                both = jnp.concatenate([label_tile(s, top, 8, tile) for s in range(slices)])
                edge_src[e, :, 128 * tile : 128 * tile + 128] = both.astype(BF16)
        for side, tile in ((0, 0), (1, per_q - 1)):
            both = jnp.concatenate([pack_edge(label_tile(s, 0, cy, tile), side == 1) for s in range(slices)])
            pack_lab[side] = both.astype(BF16)

    chunks = chunks_of(slices, cy, parts)
    il_next, il_prev = add(i, 1, n_il), add(i, -1, n_il)
    il_far = add(i, 2, n_il)

    def chunk_copy(n, way, kind, quarter):
        s, a, b = chunks[n]
        mid = middle(n, a, b)
        a, b = (a, mid) if (way == 0) == (kind != 1) else (mid, b)
        view = labs.at[quarter, s, pl.ds(a, b - a), :]
        slot = 3 * way + kind
        return remote(
            view, view, ag_send.at[n, slot], ag_recv.at[n, slot],
            dev(illum=il_next if way == 0 else il_prev),
        )

    pending = []

    def go(copy):
        copy.start()
        pending.append(copy)

    def start_chunk(copy):
        copy.start()

    def edge_copy(side):
        return remote(
            edge_src.at[side], ext.at[i, pl.ds(16 * (1 - side), 16), :], edge_send.at[side], edge_recv.at[side],
            dev(gy=add(j, 2 * side - 1, n_gy)),
        )

    def lab_col_copy(side, slot):
        return remote(
            pack_lab.at[side], ext.at[i, pl.ds(32, 16), pl.ds(128 * slot, 128)],
            cl_send.at[slot], cl_recv.at[slot], dev(gy=add(j, 1 - slot, n_gy), gx=add(g, 2 * side - 1, n_gx)),
        )

    def ext_copy(d):
        return remote(
            ext.at[i], ext.at[i], ext_send.at[d - 1], ext_recv.at[d - 1], dev(illum=add(i, d, n_il)),
        )

    def row_copy(side):
        src = inc.at[:, pl.ds(0 if side == 0 else cy - 8, 8), :]
        return remote(
            src, rowbuf.at[1 - side], row_send.at[side], row_recv.at[side], dev(gy=add(j, 2 * side - 1, n_gy))
        )

    def col_copy(side, slot):
        return remote(
            pack_fld.at[side], colbuf.at[1 - side, slot], col_send.at[side, slot], col_recv.at[side, slot],
            dev(gy=add(j, 1 - slot, n_gy), gx=add(g, 2 * side - 1, n_gx)),
        )

    def send_own(n):
        for kind in range(2):
            for way in range(2):
                start_chunk(chunk_copy(n, way, kind, i))

    def forward(n):
        for way in range(2):
            src = il_prev if way == 0 else il_next
            chunk_copy(n, way, 0, src).wait_recv()
            start_chunk(chunk_copy(n, way, 2, src))

    def arrived(n):
        for way in range(2):
            chunk_copy(n, way, 2, il_far).wait_recv()

    def near(n):
        for way in range(2):
            chunk_copy(n, way, 1, il_prev if way == 0 else il_next).wait_recv()

    up_ok, down_ok = j > 0, j < n_gy - 1
    left_ok, right_ok = g > 0, g < n_gx - 1

    def assemble_field(h):
        first = h * size
        for f in range(2):
            def main(c, carry):
                lanes = pl.ds(pl.multiple_of(c * 128, 128), 128)
                fld[f][c, 0:8, :] = jnp.zeros((8, 128), F32)
                fld[f][c, size + 24 : size + 32, :] = jnp.zeros((8, 128), F32)
                fld[f][c, 16 : size + 16, :] = stage[f, first : first + size, lanes]
                if h == 0:
                    fld[f][c, 8:16, :] = only_if(up_ok, rowbuf[0, f, :, lanes], 0.0)
                else:
                    fld[f][c, 8:16, :] = stage[f, first - 8 : first, lanes]
                if h == parts - 1:
                    fld[f][c, size + 16 : size + 24, :] = only_if(down_ok, rowbuf[1, f, :, lanes], 0.0)
                else:
                    fld[f][c, size + 16 : size + 24, :] = stage[f, first + size : first + size + 8, lanes]
                return carry

            lax.fori_loop(0, tiles, main, 0)
            fld[f][tiles, 0:8, :] = jnp.zeros((8, 128), F32)
            fld[f][tiles, size + 24 : size + 32, :] = jnp.zeros((8, 128), F32)

        def put(f, row, value):
            fld[f][tiles, row : row + 8, :] = value

        for f in range(2):
            edge_tiles(
                h, 0.0, lambda side, slot: colbuf[side, slot, f], lambda row, value: put(f, row, value)
            )

    def edge_tiles(h, fill, get, put):
        total = cy // 8
        for t in range(h * size // 8 - 1, (h + 1) * size // 8 + 1):
            slot, rank, ok = (0, total - 1, up_ok) if t < 0 else (2, 0, down_ok) if t >= total else (1, t, None)
            both = (left_ok, right_ok) if ok is None else (left_ok & ok, right_ok & ok)
            value = unpack_edges(get(0, slot), get(1, slot), rank, fill, *both)
            put(16 + 8 * t - h * size, value)

    def set_coefs(s, c, row, rows, label):
        a, b = coefficients(label)
        swing[s, c, row : row + rows, :] = a
        damp[s, c, row : row + rows, :] = b

    def quarter_coefs(s, q):
        def main(tile, carry):
            lanes = pl.ds(pl.multiple_of(tile * 128, 128), 128)
            set_coefs(s, q * per_q + tile, 16, cy, labs[q, s, :, lanes].astype(F32))
            return carry

        lax.fori_loop(0, per_q, main, 0)

    def halo_coefs(s):
        def main(c, carry):
            q = c // per_q
            lanes = pl.ds(pl.multiple_of(lax.rem(c, per_q) * 128, 128), 128)
            for row, first, ok in ((8, 0, up_ok), (cy + 16, 16, down_ok)):
                label = ext[q, first : first + 16, lanes].astype(F32)[8 * s : 8 * s + 8]
                set_coefs(s, c, row, 8, only_if(ok, label, -1.0))
            return carry

        lax.fori_loop(0, tiles, main, 0)

        def get(side, slot):
            both = ext[n_il - 1 if side == 0 else 0, 32:48, 128 * slot : 128 * slot + 128].astype(F32)
            return both[8 * s : 8 * s + 8]

        edge_tiles(0, -1.0, get, lambda row, value: set_coefs(s, tiles, row, 8, value))

    def half_step(s, target, source, sign):
        rows = (size + 16) // 2
        lane = lane_ids(rows)
        for part in range(2):
            r = 8 + rows * part
            before, mid = source[tiles, r : r + rows, :], source[0, r : r + rows, :]
            for c in range(tiles + 1):
                after = source[(c + 1) % (tiles + 1), r : r + rows, :]
                vert = source[c, r - 1 : r - 1 + rows, :] + source[c, r + 1 : r + 1 + rows, :]
                left = pltpu.roll(jnp.where(lane == 127, before, mid), 1, 1)
                right = pltpu.roll(jnp.where(lane == 0, after, mid), 127, 1)
                total = vert + (left + right) + swing[s, c, r : r + rows, :] * mid
                target[c, r : r + rows, :] = damp[s, c, r : r + rows, :] * (target[c, r : r + rows, :] + (sign * RATE) * total)
                before, mid = mid, after

    def transform(h):
        first = h * size

        def modulate(c, carry):
            lanes = pl.ds(pl.multiple_of(c * 128, 128), 128)
            cos = jnp.concatenate([turn[0, c]] * (size // 8))
            sin = jnp.concatenate([turn[1, c]] * (size // 8))
            real = fld[0][c, 16 : size + 16, :]
            imag = fld[1][c, 16 : size + 16, :]
            out_stage[0, first : first + size, lanes] = real
            out_stage[1, first : first + size, lanes] = imag
            for n, value in enumerate((real * cos - imag * sin, real * sin + imag * cos)):
                high = value.astype(BF16)
                lhs[0, n * size : (n + 1) * size, lanes] = high
                lhs[1, n * size : (n + 1) * size, lanes] = (value - high.astype(F32)).astype(BF16)
            return carry

        lax.fori_loop(0, tiles, modulate, 0)
        pltpu.make_async_copy(
            out_stage.at[:, pl.ds(first, size), :], exit_ref.at[:, pl.ds(first, size), :], sem_out.at[h]
        ).start()
        lane = lane_ids(8)
        for m in range(det // 256):
            cols = slice(256 * m, 256 * m + 256)
            prod = jnp.dot(lhs[0], wx[0, :, cols], preferred_element_type=F32)
            prod += jnp.dot(lhs[1], wx[0, :, cols], preferred_element_type=F32)
            prod += jnp.dot(lhs[0], wx[1, :, cols], preferred_element_type=F32)
            c_re, s_re = prod[:size, :128], prod[:size, 128:]
            c_im, s_im = prod[size:, :128], prod[size:, 128:]
            rank = 128 * m + lane
            for block, freq, g_re, g_im in (
                (n_gx // 2 + m, rank, c_re + s_im, c_im - s_re),
                (n_gx // 2 - 1 - m, -rank - 1, c_re - s_im, c_im + s_re),
            ):
                quarter = lax.rem((freq + det) * g, n_gx) * (4 // n_gx)
                f_re = jnp.where(quarter == 0, 1.0, jnp.where(quarter == 2, -1.0, 0.0))
                f_im = jnp.where(quarter == 1, -1.0, jnp.where(quarter == 3, 1.0, 0.0))
                f_re = jnp.concatenate([f_re] * (size // 8))
                f_im = jnp.concatenate([f_im] * (size // 8))
                value = jnp.concatenate([g_re * f_re - g_im * f_im, g_re * f_im + g_im * f_re], axis=1)
                gown[block, first : first + size, :] = value
                top = jnp.maximum(jnp.max(jnp.abs(value), axis=0, keepdims=True), 2.0**-110)
                level = jnp.ceil(jnp.log2(top) * 128.0)
                gsend[block, h, 0:16, :] = jnp.broadcast_to(level, (16, 256)).astype(jnp.int32).astype(jnp.int16)
                gsend[block, h, 16 : 16 + size, :] = (
                    jnp.round(value * (jnp.exp2(level * (-1.0 / 128.0)) * 32000.0)).astype(jnp.int32).astype(jnp.int16)
                )

            for block in (n_gx // 2 + m, n_gx // 2 - 1 - m):
                @pl.when(g != block)
                def _():
                    g_copy(h, lax.rem(block - g + n_gx, n_gx)).start()

    def g_copy(h, d):
        block = add(g, d, n_gx)
        return remote(
            gsend.at[block, h], grecv.at[d - 1, h], g_send.at[h, d - 1], g_recv.at[h, d - 1], dev(gx=block)
        )

    def g_total(h):
        total = gown[g, h * size : (h + 1) * size, :]
        for d in range(1, n_gx):
            g_copy(h, d).wait_recv()
            level = grecv[d - 1, h, 0:16, :].astype(jnp.int32).astype(F32)[0:1]
            unit = jnp.exp2(level * (1.0 / 128.0)) * (1.0 / 32000.0)
            total = total + grecv[d - 1, h, 16 : 16 + size, :].astype(jnp.int32).astype(F32) * unit
        return total

    own_labels(0)
    pl.semaphore_wait(barrier, len(peers))
    send_own(0)
    own_labels(1)
    label_edges()
    for side, owner in ((0, 0), (1, n_il - 1)):
        @pl.when(i == owner)
        def _():
            for slot in range(3):
                lab_col_copy(side, slot).start()
    for side in range(2):
        go(edge_copy(side))
    for side in range(2):
        go(row_copy(side))
    load_fld.wait()
    for f in range(2):
        pack_fld[0, f] = pack_edge(stage[f, :, 0:128], False)
        pack_fld[1, f] = pack_edge(stage[f, :, cx - 128 : cx], True)
    for side in range(2):
        for slot in range(3):
            go(col_copy(side, slot))
    forward(0)
    for side in range(2):
        edge_copy(side).wait_recv()
    @pl.when((i == 0) | (i == n_il - 1))
    def _():
        for slot in range(3):
            lab_col_copy(0, slot).wait_recv()
    for d in range(1, n_il):
        go(ext_copy(d))
    send_own(1)
    quarter_coefs(0, i)
    quarter_coefs(1, i)
    near(0)
    quarter_coefs(0, il_prev)
    quarter_coefs(0, il_next)
    for side in range(2):
        row_copy(side).wait_recv()
        for slot in range(3):
            col_copy(side, slot).wait_recv()
    assemble_field(0)
    for d in range(1, n_il):
        ext_copy(d).wait_recv()
    for s in range(slices):
        halo_coefs(s)
    arrived(0)
    quarter_coefs(0, il_far)
    for s in range(slices):
        def substep(step, carry):
            if s == 0:
                @pl.when(step == 1)
                def _():
                    forward(1)

            half_step(s, fld[0], fld[1], -1.0)
            half_step(s, fld[1], fld[0], 1.0)
            return carry

        lax.fori_loop(0, SUB, substep, 0)
        if s == 0:
            near(1)
            quarter_coefs(1, il_prev)
            quarter_coefs(1, il_next)
            arrived(1)
            quarter_coefs(1, il_far)
    load_turn.wait()
    load_wx.wait()
    transform(0)

    load_ey.wait()
    for h in range(parts):
        total = g_total(h)
        high = total.astype(BF16)
        low = (total - high.astype(F32)).astype(BF16)
        rows = slice(h * size, (h + 1) * size)
        for n, value in enumerate((high, low)):
            rhs[n, rows, :] = value
            rhs[n, cy + h * size : cy + (h + 1) * size, 0:128] = value[:, 128:256]
            rhs[n, cy + h * size : cy + (h + 1) * size, 128:256] = -value[:, 0:128]

    share = det // n_gy
    half = det // 2
    odd = lax.rem(j, 2)

    def wave_rows(parity):
        rows = pl.ds(pl.multiple_of(parity * half, half), half)
        return (
            jnp.dot(ey[0, rows, :], rhs[0], preferred_element_type=F32)
            + jnp.dot(ey[1, rows, :], rhs[0], preferred_element_type=F32)
            + jnp.dot(ey[0, rows, :], rhs[1], preferred_element_type=F32)
        )

    fsend[...] = wave_rows(1 - odd)
    pair = remote(fsend, fpair, pair_sem.at[0], pair_sem.at[1], dev(gy=j + 1 - 2 * odd))
    go(pair)
    own = wave_rows(odd)
    pair.wait_recv()
    fhalf[...] = own + fpair[...]

    def f_copy(d):
        there = add(j, d, n_gy)
        return remote(
            fhalf.at[pl.ds(pl.multiple_of(there // 2 * share, share), share), :], frecv.at[d // 2 - 1],
            f_send.at[d // 2 - 1], f_recv.at[d // 2 - 1], dev(gy=there),
        )

    for d in range(2, n_gy, 2):
        go(f_copy(d))
    acc = fhalf[pl.ds(pl.multiple_of(j // 2 * share, share), share), :]
    for d in range(2, n_gy, 2):
        f_copy(d).wait_recv()
        acc = acc + frecv[d // 2 - 1]
    row_id = lax.broadcasted_iota(jnp.int32, (128, 128), 0)
    col_id = lax.broadcasted_iota(jnp.int32, (128, 128), 1)
    mirror = jnp.full((128, 128), (g < n_gx // 2).astype(jnp.int32), jnp.int32)
    order = jnp.where(jnp.where(mirror > 0, 127 - col_id, col_id) == row_id, 1.0, 0.0)
    for n in range(2):
        far_ref[n] = jnp.dot(
            acc[:, 128 * n : 128 * n + 128], order, precision=lax.Precision.HIGHEST, preferred_element_type=F32
        )

    for copy in pending:
        copy.wait_send()
    for n in range(len(chunks)):
        for way in range(2):
            for kind in range(3):
                chunk_copy(n, way, kind, i).wait_send()
    for h in range(parts):
        for d in range(1, n_gx):
            g_copy(h, d).wait_send()
    @pl.when((i == 0) | (i == n_il - 1))
    def _():
        for slot in range(3):
            lab_col_copy(0, slot).wait_send()
    for h in range(parts):
        rows = pl.ds(h * size, size)
        pltpu.make_async_copy(out_stage.at[:, rows, :], exit_ref.at[:, rows, :], sem_out.at[h]).wait()


def on_device(dims, det, incident, labels):
    n_il, n_gy, n_gx = dims
    slices, cy = labels.shape[:2]
    hbm_spec = pl.BlockSpec(memory_space=pltpu.HBM)
    qx = labels.shape[4]
    cx = incident.shape[3]
    ny, nx = cy * n_gy, cx * n_gx
    wave_x, turn, wave_y = tables(det, cy, cx, ny, nx)
    tiles = cx // 128
    size = cy // PARTS
    share = det // n_gy
    n_chunks = len(chunks_of(slices, cy, PARTS))
    dma = pltpu.SemaphoreType.DMA
    vmem = pltpu.VMEM
    any_spec = pl.BlockSpec(memory_space=pl.ANY)
    vmem_spec = pl.BlockSpec(memory_space=pltpu.VMEM)
    field, far = pl.pallas_call(
        functools.partial(kernel, dims),
        out_shape=(
            pltpu.VMEM((2, cy, cx), F32),
            pltpu.VMEM((2, share, 128), F32),
        ),
        in_specs=[hbm_spec] * 5,
        out_specs=(any_spec, vmem_spec),
        scratch_shapes=[
            vmem((slices * cy * qx // 128, 128), jnp.int32),
            vmem((2, cy, cx), F32),
            vmem((2, cy, cx), F32),
            vmem((n_il, slices, cy, qx), BF16),
            vmem((2, 8 * slices, qx), BF16),
            vmem((2, 8 * slices, 128), BF16),
            vmem((n_il, 24 * slices, qx), BF16),
            vmem((2, 2, 8, cx), F32),
            vmem((2, 2, 8, 128), F32),
            vmem((2, 3, 2, 8, 128), F32),
            vmem((tiles + 1, size + 32, 128), F32),
            vmem((tiles + 1, size + 32, 128), F32),
            vmem((slices, tiles + 1, size + 32, 128), F32),
            vmem((slices, tiles + 1, size + 32, 128), F32),
            vmem((2, tiles, 8, 128), F32),
            vmem((2, 2 * size, cx), BF16),
            vmem((2, cx, det), BF16),
            vmem((2, det, 2 * cy), BF16),
            vmem((n_gx, cy, 256), F32),
            vmem((n_gx, PARTS, 16 + size, 256), jnp.int16),
            vmem((n_gx - 1, PARTS, 16 + size, 256), jnp.int16),
            vmem((2, 2 * cy, 256), BF16),
            vmem((det // 2, 256), F32),
            vmem((det // 2, 256), F32),
            vmem((det // 2, 256), F32),
            vmem((n_gy // 2 - 1, share, 256), F32),
            dma((slices,)),
            dma((5,)),
            dma((PARTS,)),
            dma((n_chunks, 6)),
            dma((n_chunks, 6)),
            dma((2,)),
            dma((2,)),
            dma((3,)),
            dma((3,)),
            dma((n_il - 1,)),
            dma((n_il - 1,)),
            dma((2,)),
            dma((2,)),
            dma((2, 3)),
            dma((2, 3)),
            dma((PARTS, n_gx - 1)),
            dma((PARTS, n_gx - 1)),
            dma((2,)),
            dma((n_gy // 2 - 1,)),
            dma((n_gy // 2 - 1,)),
        ],
        compiler_params=pltpu.CompilerParams(
            collective_id=0, has_side_effects=True, vmem_limit_bytes=48 * 1024 * 1024
        ),
    )(
        *(
            pltpu.with_memory_space_constraint(x, pltpu.HBM)
            for x in (
                incident.reshape(2, cy, cx),
                labels.reshape(slices * cy * qx // 128, 128),
                jnp.asarray(wave_x),
                jnp.asarray(wave_y),
                jnp.asarray(turn),
            )
        )
    )
    return field[None], far[None]


def solution(mesh, det=DET):
    dims = tuple(mesh.shape[name] for name in ("illum", "gy", "gx"))
    in_specs = (P("illum", None, "gy", "gx"), P(None, "gy", "gx", "illum", None))
    out_specs = (P("illum", None, "gy", "gx"), P("illum", None, "gy", "gx"))
    return jax.shard_map(
        functools.partial(on_device, dims, det), mesh=mesh, in_specs=in_specs, out_specs=out_specs, check_vma=False
    )
```

time: 63.3 us -> 52 us (0.82)
  Pallas kernels: 57 us -> 49.4 us
  local copies, waits for them, and re-layouts: 5.5 us -> 1.94 us
    pallas_call x1, Pallas kernels: 57 us -> 49.4 us  [on_device(): pl.pallas_call(functools.partial(kernel, dims), out_shape=(pltpu.VMEM((2,...]
    unnamed x7 -> x2, local copies, waits for them, and re-layouts: 5.5 us -> 1.94 us
where the time goes in v3:
time: 52 us; the launch traced here: 51.9 us
  Pallas kernels  49.4 us (95%)
  local copies, waits for them, and re-layouts  1.94 us (4%)
  between operations  0.64 us (1%)
    pallas_call x1, Pallas kernels, on_device(): pl.pallas_call(functools.partial(kernel, dims), out_shape=(pltpu.VMEM((2,...  49.4 us
    unnamed x2, local copies, waits for them, and re-layouts  1.94 us

profile of v3, /device:TPU:1, one launch (start us, length us, event | category | flops | bytes accessed | tf_op | source)
XLA Modules:
  0.0 51.9 jit_solution(13827419908595358316)
XLA Ops:
  0.6 49.4 %shard_map.68 = (f32[2,128,2048]{2,1,0:T(8,128)S(1)}, f32[2,32,128]{2,1,0:T(8,128)S(1)}) custom-call(f32[2,128,2048]{2,1,0:T(8,128)} %bitcast.6, s32[1024,128]{1,0:T(8,128)} %bitcast.7, bf16[2,2048,512]{2,1,0:T(8,128)(2,1)} %constant.6.clone.wx_hbm, bf16[16,2,512,256]{3,2,1,0:T(8,128)(2,1)} %constant.7.clone.ey_hbm, f32[2,16,8,128]{3,2,1,0:T(8,128)} %constant.8.clone.turn_hbm), custom_call_target="tpu_custom_call" | custom-call | tf_op jit(solution)/shard_map/pallas_call | solution.py:564
  50.0 1.3 %copy.9 = f32[1,2,128,2048]{3,2,1,0:T(8,128)} copy(f32[1,2,128,2048]{3,2,1,0:T(8,128)S(1)} %bitcast.4) | data formatting | bytes 4194304
  51.3 0.6 %copy.10 = f32[1,2,32,128]{3,2,1,0:T(8,128)} copy(f32[1,2,32,128]{3,2,1,0:T(8,128)S(1)} %bitcast.5) | data formatting | bytes 65536

commit v4 on v3

--- a/solution.py
+++ b/solution.py
@@ -87,6 +87,26 @@
     return swing, damp
 
 
+def encode(real, imag):
+    levels, bodies = [], []
+    for value in (real, imag):
+        top = jnp.maximum(jnp.max(jnp.abs(value), axis=0, keepdims=True), 2.0**-110)
+        level = jnp.ceil(jnp.log2(top) * 128.0)
+        levels.append(level)
+        bodies.append(jnp.round(value * (jnp.exp2(level * (-1.0 / 128.0)) * 32000.0)).astype(jnp.int32).astype(jnp.int16))
+    row = lax.broadcasted_iota(jnp.int32, (16, 128), 0)
+    shape = (16, 128)
+    head = jnp.where(row == 0, jnp.broadcast_to(levels[0], shape), jnp.broadcast_to(levels[1], shape))
+    return head.astype(jnp.int32).astype(jnp.int16), bodies[0], bodies[1]
+
+
+def decode(block, rows):
+    unit = jnp.exp2(block[0:16].astype(jnp.int32).astype(F32) * (1.0 / 128.0)) * (1.0 / 32000.0)
+    return [
+        block[16 + n * rows : 16 + (n + 1) * rows].astype(jnp.int32).astype(F32) * unit[n : n + 1] for n in range(2)
+    ]
+
+
 def chunks_of(slices, cy, parts):
     if parts == 1:
         return [(s, 0, cy) for s in range(slices)]
@@ -102,9 +122,9 @@
 def kernel(
     dims, inc, lab, wx_hbm, ey_hbm, turn_hbm, exit_ref, far_ref,
     lab_in, stage, out_stage, labs, edge_src, pack_lab, ext, rowbuf, pack_fld, colbuf,
-    fld_re, fld_im, swing, damp, turn, lhs, wx, ey, gown, gsend, grecv, rhs, fsend, fpair, fhalf, frecv,
-    sem_lab, sem_in, sem_out, ag_send, ag_recv, edge_send, edge_recv, cl_send, cl_recv, ext_send, ext_recv,
-    row_send, row_recv, col_send, col_recv, g_send, g_recv, pair_sem, f_send, f_recv,
+    fld_re, fld_im, swing, damp, turn, lhs, wx, ey, gown, gsend, grecv, rhs, fsend, fpair, fhalf, fcode, frecv,
+    sem_lab, sem_in, sem_out, ag_send, ag_recv, edge_send, edge_recv, cl_send, cl_recv, ext_send, ext_recv, extc_send, extc_recv,
+    row_send, row_recv, col_send, col_recv, g_send, g_recv, pair_send, pair_recv, f_send, f_recv,
 ):
     n_il, n_gy, n_gx = dims
     fld = (fld_re, fld_im)
@@ -147,7 +167,6 @@
     for load in load_lab:
         load.start()
     load_fld.start()
-    ext[i, 32:48, :] = jnp.zeros((16, qx), BF16)
 
     barrier = pltpu.get_barrier_semaphore()
     peers = [dev(illum=add(i, d, n_il)) for d in range(1, n_il)]
@@ -217,8 +236,13 @@
         )
 
     def ext_copy(d):
-        return remote(
-            ext.at[i], ext.at[i], ext_send.at[d - 1], ext_recv.at[d - 1], dev(illum=add(i, d, n_il)),
+        view = ext.at[i, pl.ds(0, 32), :]
+        return remote(view, view, ext_send.at[d - 1], ext_recv.at[d - 1], dev(illum=add(i, d, n_il)))
+
+    def ext_col_copy(d, source):
+        view = ext.at[source, pl.ds(32, 16), pl.ds(0, 384)]
+        return remote(
+            view, view, extc_send.at[d - 1], extc_recv.at[lax.rem(source, 2)], dev(illum=add(i, d, n_il))
         )
 
     def row_copy(side):
@@ -360,8 +384,10 @@
             out_stage.at[:, pl.ds(first, size), :], exit_ref.at[:, pl.ds(first, size), :], sem_out.at[h]
         ).start()
         lane = lane_ids(8)
-        for m in range(det // 256):
-            cols = slice(256 * m, 256 * m + 256)
+        first_m = jnp.where((g == 0) | (g == n_gx - 1), 0, 1)
+        for turn_no in range(det // 256):
+            m = first_m + turn_no - 2 * first_m * turn_no
+            cols = pl.ds(pl.multiple_of(256 * m, 256), 256)
             prod = jnp.dot(lhs[0], wx[0, :, cols], preferred_element_type=F32)
             prod += jnp.dot(lhs[1], wx[0, :, cols], preferred_element_type=F32)
             prod += jnp.dot(lhs[0], wx[1, :, cols], preferred_element_type=F32)
@@ -377,19 +403,22 @@
                 f_im = jnp.where(quarter == 1, -1.0, jnp.where(quarter == 3, 1.0, 0.0))
                 f_re = jnp.concatenate([f_re] * (size // 8))
                 f_im = jnp.concatenate([f_im] * (size // 8))
-                value = jnp.concatenate([g_re * f_re - g_im * f_im, g_re * f_im + g_im * f_re], axis=1)
-                gown[block, first : first + size, :] = value
-                top = jnp.maximum(jnp.max(jnp.abs(value), axis=0, keepdims=True), 2.0**-110)
-                level = jnp.ceil(jnp.log2(top) * 128.0)
-                gsend[block, h, 0:16, :] = jnp.broadcast_to(level, (16, 256)).astype(jnp.int32).astype(jnp.int16)
-                gsend[block, h, 16 : 16 + size, :] = (
-                    jnp.round(value * (jnp.exp2(level * (-1.0 / 128.0)) * 32000.0)).astype(jnp.int32).astype(jnp.int16)
-                )
-
-            for block in (n_gx // 2 + m, n_gx // 2 - 1 - m):
-                @pl.when(g != block)
-                def _():
-                    g_copy(h, lax.rem(block - g + n_gx, n_gx)).start()
+                real, imag = g_re * f_re - g_im * f_im, g_re * f_im + g_im * f_re
+                gown[block, 0:size, :] = real
+                gown[block, size : 2 * size, :] = imag
+                head, real, imag = encode(real, imag)
+                gsend[block, h, 0:16, :] = head
+                gsend[block, h, 16 : 16 + size, :] = real
+                gsend[block, h, 16 + size : 16 + 2 * size, :] = imag
+            opposite = add(g, 2, n_gx)
+            if turn_no == 0:
+                g_copy(h, 2).start()
+                other = 2 * (n_gx // 2) - 1 - opposite
+            else:
+                other = 2 * (n_gx // 2) - 1 - g
+            @pl.when(other != g)
+            def _():
+                g_copy(h, lax.rem(other - g + n_gx, n_gx)).start()
 
     def g_copy(h, d):
         block = add(g, d, n_gx)
@@ -398,13 +427,12 @@
         )
 
     def g_total(h):
-        total = gown[g, h * size : (h + 1) * size, :]
+        real, imag = gown[g, 0:size, :], gown[g, size : 2 * size, :]
         for d in range(1, n_gx):
             g_copy(h, d).wait_recv()
-            level = grecv[d - 1, h, 0:16, :].astype(jnp.int32).astype(F32)[0:1]
-            unit = jnp.exp2(level * (1.0 / 128.0)) * (1.0 / 32000.0)
-            total = total + grecv[d - 1, h, 16 : 16 + size, :].astype(jnp.int32).astype(F32) * unit
-        return total
+            more = decode(grecv[d - 1, h], size)
+            real, imag = real + more[0], imag + more[1]
+        return real, imag
 
     own_labels(0)
     pl.semaphore_wait(barrier, len(peers))
@@ -434,6 +462,8 @@
     def _():
         for slot in range(3):
             lab_col_copy(0, slot).wait_recv()
+        for d in range(1, n_il):
+            ext_col_copy(d, i).start()
     for d in range(1, n_il):
         go(ext_copy(d))
     send_own(1)
@@ -449,6 +479,10 @@
     assemble_field(0)
     for d in range(1, n_il):
         ext_copy(d).wait_recv()
+    for owner in (0, n_il - 1):
+        @pl.when(i != owner)
+        def _():
+            ext_col_copy(1, owner).wait_recv()
     for s in range(slices):
         halo_coefs(s)
     arrived(0)
@@ -477,14 +511,15 @@
 
     load_ey.wait()
     for h in range(parts):
-        total = g_total(h)
-        high = total.astype(BF16)
-        low = (total - high.astype(F32)).astype(BF16)
-        rows = slice(h * size, (h + 1) * size)
-        for n, value in enumerate((high, low)):
-            rhs[n, rows, :] = value
-            rhs[n, cy + h * size : cy + (h + 1) * size, 0:128] = value[:, 128:256]
-            rhs[n, cy + h * size : cy + (h + 1) * size, 128:256] = -value[:, 0:128]
+        for col, value in enumerate(g_total(h)):
+            high = value.astype(BF16)
+            low = (value - high.astype(F32)).astype(BF16)
+            for n, piece in enumerate((high, low)):
+                rhs[n, 0:cy, 128 * col : 128 * col + 128] = piece
+                if col == 0:
+                    rhs[n, cy : 2 * cy, 128:256] = -piece
+                else:
+                    rhs[n, cy : 2 * cy, 0:128] = piece
 
     share = det // n_gy
     half = det // 2
@@ -498,33 +533,48 @@
             + jnp.dot(ey[0, rows, :], rhs[1], preferred_element_type=F32)
         )
 
+    def pair_copy(k):
+        rows = pl.ds(k * half // 2, half // 2)
+        return remote(
+            fsend.at[rows, :], fpair.at[rows, :], pair_send.at[k], pair_recv.at[k], dev(gy=j + 1 - 2 * odd)
+        )
+
     fsend[...] = wave_rows(1 - odd)
-    pair = remote(fsend, fpair, pair_sem.at[0], pair_sem.at[1], dev(gy=j + 1 - 2 * odd))
-    go(pair)
-    own = wave_rows(odd)
-    pair.wait_recv()
-    fhalf[...] = own + fpair[...]
+    for k in range(2):
+        go(pair_copy(k))
+    fhalf[...] = wave_rows(odd)
+    for k in range(2):
+        pair_copy(k).wait_recv()
+    fhalf[...] += fpair[...]
+    head, real, imag = encode(fhalf[:, 0:128], fhalf[:, 128:256])
+    for k in range(n_gy // 2):
+        rows = slice(k * share, (k + 1) * share)
+        fcode[k, 0:16, :] = head
+        fcode[k, 16 : 16 + share, :] = real[rows]
+        fcode[k, 16 + share : 16 + 2 * share, :] = imag[rows]
 
     def f_copy(d):
         there = add(j, d, n_gy)
         return remote(
-            fhalf.at[pl.ds(pl.multiple_of(there // 2 * share, share), share), :], frecv.at[d // 2 - 1],
-            f_send.at[d // 2 - 1], f_recv.at[d // 2 - 1], dev(gy=there),
-        )
-
-    for d in range(2, n_gy, 2):
+            fcode.at[there // 2], frecv.at[d // 2 - 1], f_send.at[d // 2 - 1], f_recv.at[d // 2 - 1], dev(gy=there)
+        )
+
+    order = sorted(range(2, n_gy, 2), key=lambda d: (abs(d - n_gy // 2), d))
+    for d in order:
         go(f_copy(d))
-    acc = fhalf[pl.ds(pl.multiple_of(j // 2 * share, share), share), :]
-    for d in range(2, n_gy, 2):
+    own = pl.ds(pl.multiple_of(j // 2 * share, share), share)
+    acc = [fhalf[own, 0:128], fhalf[own, 128:256]]
+    for d in order:
         f_copy(d).wait_recv()
-        acc = acc + frecv[d // 2 - 1]
+        more = decode(frecv[d // 2 - 1], share)
+        acc = [acc[0] + more[0], acc[1] + more[1]]
     row_id = lax.broadcasted_iota(jnp.int32, (128, 128), 0)
     col_id = lax.broadcasted_iota(jnp.int32, (128, 128), 1)
     mirror = jnp.full((128, 128), (g < n_gx // 2).astype(jnp.int32), jnp.int32)
-    order = jnp.where(jnp.where(mirror > 0, 127 - col_id, col_id) == row_id, 1.0, 0.0)
+    places = jnp.where(jnp.where(mirror > 0, 127 - col_id, col_id) == row_id, 1.0, 0.0)
     for n in range(2):
         far_ref[n] = jnp.dot(
-            acc[:, 128 * n : 128 * n + 128], order, precision=lax.Precision.HIGHEST, preferred_element_type=F32
+            acc[n], places, precision=lax.Precision.HIGHEST, preferred_element_type=F32
         )
 
     for copy in pending:
@@ -540,6 +590,8 @@
     def _():
         for slot in range(3):
             lab_col_copy(0, slot).wait_send()
+        for d in range(1, n_il):
+            ext_col_copy(d, i).wait_send()
     for h in range(parts):
         rows = pl.ds(h * size, size)
         pltpu.make_async_copy(out_stage.at[:, rows, :], exit_ref.at[:, rows, :], sem_out.at[h]).wait()
@@ -588,14 +640,15 @@
             vmem((2, 2 * size, cx), BF16),
             vmem((2, cx, det), BF16),
             vmem((2, det, 2 * cy), BF16),
-            vmem((n_gx, cy, 256), F32),
-            vmem((n_gx, PARTS, 16 + size, 256), jnp.int16),
-            vmem((n_gx - 1, PARTS, 16 + size, 256), jnp.int16),
+            vmem((n_gx, 2 * cy, 128), F32),
+            vmem((n_gx, PARTS, 16 + 2 * size, 128), jnp.int16),
+            vmem((n_gx - 1, PARTS, 16 + 2 * size, 128), jnp.int16),
             vmem((2, 2 * cy, 256), BF16),
             vmem((det // 2, 256), F32),
             vmem((det // 2, 256), F32),
             vmem((det // 2, 256), F32),
-            vmem((n_gy // 2 - 1, share, 256), F32),
+            vmem((n_gy // 2, 16 + 2 * share, 128), jnp.int16),
+            vmem((n_gy // 2 - 1, 16 + 2 * share, 128), jnp.int16),
             dma((slices,)),
             dma((5,)),
             dma((PARTS,)),
@@ -607,12 +660,15 @@
             dma((3,)),
             dma((n_il - 1,)),
             dma((n_il - 1,)),
+            dma((n_il - 1,)),
+            dma((2,)),
             dma((2,)),
             dma((2,)),
             dma((2, 3)),
             dma((2, 3)),
             dma((PARTS, n_gx - 1)),
             dma((PARTS, n_gx - 1)),
+            dma((2,)),
             dma((2,)),
             dma((n_gy // 2 - 1,)),
             dma((n_gy // 2 - 1,)),

time: 52 us -> 49.8 us (0.958)
  Pallas kernels: 49.4 us -> 47.2 us
    pallas_call x1, Pallas kernels: 49.4 us -> 47.2 us  [on_device(): pl.pallas_call(functools.partial(kernel, dims), out_shape=(pltpu.VMEM((2,...]
where the time goes in v4:
time: 49.8 us; the launch traced here: 49.7 us
  Pallas kernels  47.2 us (95%)
  local copies, waits for them, and re-layouts  1.94 us (4%)
  between operations  0.64 us (1%)
    pallas_call x1, Pallas kernels, on_device(): pl.pallas_call(functools.partial(kernel, dims), out_shape=(pltpu.VMEM((2,...  47.2 us
    unnamed x2, local copies, waits for them, and re-layouts  1.94 us

profile of v4, /device:TPU:1, one launch (start us, length us, event | category | flops | bytes accessed | tf_op | source)
XLA Modules:
  0.0 49.7 jit_solution(7655699574476243783)
XLA Ops:
  0.6 47.2 %shard_map.68 = (f32[2,128,2048]{2,1,0:T(8,128)S(1)}, f32[2,32,128]{2,1,0:T(8,128)S(1)}) custom-call(f32[2,128,2048]{2,1,0:T(8,128)} %bitcast.6, s32[1024,128]{1,0:T(8,128)} %bitcast.7, bf16[2,2048,512]{2,1,0:T(8,128)(2,1)} %constant.6.clone.wx_hbm, bf16[16,2,512,256]{3,2,1,0:T(8,128)(2,1)} %constant.7.clone.ey_hbm, f32[2,16,8,128]{3,2,1,0:T(8,128)} %constant.8.clone.turn_hbm), custom_call_target="tpu_custom_call" | custom-call | tf_op jit(solution)/shard_map/pallas_call | solution.py:616
  47.8 1.3 %copy.9 = f32[1,2,128,2048]{3,2,1,0:T(8,128)} copy(f32[1,2,128,2048]{3,2,1,0:T(8,128)S(1)} %bitcast.4) | data formatting | bytes 4194304
  49.1 0.6 %copy.10 = f32[1,2,32,128]{3,2,1,0:T(8,128)} copy(f32[1,2,32,128]{3,2,1,0:T(8,128)S(1)} %bitcast.5) | data formatting | bytes 65536

commit v5 on v4

--- a/solution.py
+++ b/solution.py
@@ -477,29 +477,25 @@
         for slot in range(3):
             col_copy(side, slot).wait_recv()
     assemble_field(0)
+    arrived(0)
+    quarter_coefs(0, il_far)
     for d in range(1, n_il):
         ext_copy(d).wait_recv()
     for owner in (0, n_il - 1):
         @pl.when(i != owner)
         def _():
             ext_col_copy(1, owner).wait_recv()
-    for s in range(slices):
-        halo_coefs(s)
-    arrived(0)
-    quarter_coefs(0, il_far)
+    halo_coefs(0)
+    forward(1)
     for s in range(slices):
         def substep(step, carry):
-            if s == 0:
-                @pl.when(step == 1)
-                def _():
-                    forward(1)
-
             half_step(s, fld[0], fld[1], -1.0)
             half_step(s, fld[1], fld[0], 1.0)
             return carry
 
         lax.fori_loop(0, SUB, substep, 0)
         if s == 0:
+            halo_coefs(1)
             near(1)
             quarter_coefs(1, il_prev)
             quarter_coefs(1, il_next)

time: 49.8 us -> 48.4 us (0.972)
  Pallas kernels: 47.2 us -> 45.7 us
    pallas_call x1, Pallas kernels: 47.2 us -> 45.7 us  [on_device(): pl.pallas_call(functools.partial(kernel, dims), out_shape=(pltpu.VMEM((2,...]
where the time goes in v5:
time: 48.4 us; the launch traced here: 48.3 us
  Pallas kernels  45.7 us (94%)
  local copies, waits for them, and re-layouts  1.94 us (4%)
  between operations  0.64 us (1%)
    pallas_call x1, Pallas kernels, on_device(): pl.pallas_call(functools.partial(kernel, dims), out_shape=(pltpu.VMEM((2,...  45.7 us
    unnamed x2, local copies, waits for them, and re-layouts  1.94 us

profile of v5, /device:TPU:1, one launch (start us, length us, event | category | flops | bytes accessed | tf_op | source)
XLA Modules:
  0.0 48.3 jit_solution(11711780402282781923)
XLA Ops:
  0.6 45.7 %shard_map.68 = (f32[2,128,2048]{2,1,0:T(8,128)S(1)}, f32[2,32,128]{2,1,0:T(8,128)S(1)}) custom-call(f32[2,128,2048]{2,1,0:T(8,128)} %bitcast.6, s32[1024,128]{1,0:T(8,128)} %bitcast.7, bf16[2,2048,512]{2,1,0:T(8,128)(2,1)} %constant.6.clone.wx_hbm, bf16[16,2,512,256]{3,2,1,0:T(8,128)(2,1)} %constant.7.clone.ey_hbm, f32[2,16,8,128]{3,2,1,0:T(8,128)} %constant.8.clone.turn_hbm), custom_call_target="tpu_custom_call" | custom-call | tf_op jit(solution)/shard_map/pallas_call | solution.py:612
  46.4 1.3 %copy.9 = f32[1,2,128,2048]{3,2,1,0:T(8,128)} copy(f32[1,2,128,2048]{3,2,1,0:T(8,128)S(1)} %bitcast.4) | data formatting | bytes 4194304
  47.7 0.6 %copy.10 = f32[1,2,32,128]{3,2,1,0:T(8,128)} copy(f32[1,2,32,128]{3,2,1,0:T(8,128)S(1)} %bitcast.5) | data formatting | bytes 65536

commit v6 on v5

--- a/solution.py
+++ b/solution.py
@@ -282,17 +282,19 @@
     def assemble_field(h):
         first = h * size
         for f in range(2):
+            rate = RATE if f else 1.0
+
             def main(c, carry):
                 lanes = pl.ds(pl.multiple_of(c * 128, 128), 128)
                 fld[f][c, 0:8, :] = jnp.zeros((8, 128), F32)
                 fld[f][c, size + 24 : size + 32, :] = jnp.zeros((8, 128), F32)
-                fld[f][c, 16 : size + 16, :] = stage[f, first : first + size, lanes]
+                fld[f][c, 16 : size + 16, :] = stage[f, first : first + size, lanes] * rate
                 if h == 0:
-                    fld[f][c, 8:16, :] = only_if(up_ok, rowbuf[0, f, :, lanes], 0.0)
+                    fld[f][c, 8:16, :] = only_if(up_ok, rowbuf[0, f, :, lanes], 0.0) * rate
                 else:
                     fld[f][c, 8:16, :] = stage[f, first - 8 : first, lanes]
                 if h == parts - 1:
-                    fld[f][c, size + 16 : size + 24, :] = only_if(down_ok, rowbuf[1, f, :, lanes], 0.0)
+                    fld[f][c, size + 16 : size + 24, :] = only_if(down_ok, rowbuf[1, f, :, lanes], 0.0) * rate
                 else:
                     fld[f][c, size + 16 : size + 24, :] = stage[f, first + size : first + size + 8, lanes]
                 return carry
@@ -306,7 +308,7 @@
 
         for f in range(2):
             edge_tiles(
-                h, 0.0, lambda side, slot: colbuf[side, slot, f], lambda row, value: put(f, row, value)
+                h, 0.0, lambda side, slot: colbuf[side, slot, f], lambda row, value: put(f, row, value * (RATE if f else 1.0))
             )
 
     def edge_tiles(h, fill, get, put):
@@ -347,19 +349,23 @@
 
         edge_tiles(0, -1.0, get, lambda row, value: set_coefs(s, tiles, row, 8, value))
 
-    def half_step(s, target, source, sign):
-        rows = (size + 16) // 2
+    def half_step(s, target, source, sign, last=False):
+        rows = (size if last else size + 16) // 2
         lane = lane_ids(rows)
         for part in range(2):
-            r = 8 + rows * part
+            r = (16 if last else 8) + rows * part
             before, mid = source[tiles, r : r + rows, :], source[0, r : r + rows, :]
-            for c in range(tiles + 1):
+            for c in range(tiles if last else tiles + 1):
                 after = source[(c + 1) % (tiles + 1), r : r + rows, :]
                 vert = source[c, r - 1 : r - 1 + rows, :] + source[c, r + 1 : r + 1 + rows, :]
                 left = pltpu.roll(jnp.where(lane == 127, before, mid), 1, 1)
                 right = pltpu.roll(jnp.where(lane == 0, after, mid), 127, 1)
                 total = vert + (left + right) + swing[s, c, r : r + rows, :] * mid
-                target[c, r : r + rows, :] = damp[s, c, r : r + rows, :] * (target[c, r : r + rows, :] + (sign * RATE) * total)
+                target[c, r : r + rows, :] = (
+                    damp[s, c, r : r + rows, :] * (
+                        target[c, r : r + rows, :] + (RATE * RATE) * total if sign > 0 else target[c, r : r + rows, :] - total
+                    )
+                )
                 before, mid = mid, after
 
     def transform(h):
@@ -370,7 +376,7 @@
             cos = jnp.concatenate([turn[0, c]] * (size // 8))
             sin = jnp.concatenate([turn[1, c]] * (size // 8))
             real = fld[0][c, 16 : size + 16, :]
-            imag = fld[1][c, 16 : size + 16, :]
+            imag = fld[1][c, 16 : size + 16, :] * (1.0 / RATE)
             out_stage[0, first : first + size, lanes] = real
             out_stage[1, first : first + size, lanes] = imag
             for n, value in enumerate((real * cos - imag * sin, real * sin + imag * cos)):
@@ -488,12 +494,9 @@
     halo_coefs(0)
     forward(1)
     for s in range(slices):
-        def substep(step, carry):
+        for step in range(SUB):
             half_step(s, fld[0], fld[1], -1.0)
-            half_step(s, fld[1], fld[0], 1.0)
-            return carry
-
-        lax.fori_loop(0, SUB, substep, 0)
+            half_step(s, fld[1], fld[0], 1.0, s == slices - 1 and step == SUB - 1)
         if s == 0:
             halo_coefs(1)
             near(1)

time: 48.4 us -> 48.1 us (level)
  no operation moved by 1% of the time
where the time goes in v6:
time: 48.1 us; the launch traced here: 48 us
  Pallas kernels  45.4 us (94%)
  local copies, waits for them, and re-layouts  1.94 us (4%)
  between operations  0.64 us (1%)
    pallas_call x1, Pallas kernels, on_device(): pl.pallas_call(functools.partial(kernel, dims), out_shape=(pltpu.VMEM((2,...  45.4 us
    unnamed x2, local copies, waits for them, and re-layouts  1.94 us

profile of v6, /device:TPU:1, one launch (start us, length us, event | category | flops | bytes accessed | tf_op | source)
XLA Modules:
  0.0 48.0 jit_solution(9023570859087893758)
XLA Ops:
  0.6 45.4 %shard_map.68 = (f32[2,128,2048]{2,1,0:T(8,128)S(1)}, f32[2,32,128]{2,1,0:T(8,128)S(1)}) custom-call(f32[2,128,2048]{2,1,0:T(8,128)} %bitcast.6, s32[1024,128]{1,0:T(8,128)} %bitcast.7, bf16[2,2048,512]{2,1,0:T(8,128)(2,1)} %constant.6.clone.wx_hbm, bf16[16,2,512,256]{3,2,1,0:T(8,128)(2,1)} %constant.7.clone.ey_hbm, f32[2,16,8,128]{3,2,1,0:T(8,128)} %constant.8.clone.turn_hbm), custom_call_target="tpu_custom_call" | custom-call | tf_op jit(solution)/shard_map/pallas_call | solution.py:615
  46.1 1.3 %copy.9 = f32[1,2,128,2048]{3,2,1,0:T(8,128)} copy(f32[1,2,128,2048]{3,2,1,0:T(8,128)S(1)} %bitcast.4) | data formatting | bytes 4194304
  47.4 0.6 %copy.10 = f32[1,2,32,128]{3,2,1,0:T(8,128)} copy(f32[1,2,32,128]{3,2,1,0:T(8,128)S(1)} %bitcast.5) | data formatting | bytes 65536

commit v7 on v6

--- a/solution.py
+++ b/solution.py
@@ -621,7 +621,7 @@
         in_specs=[hbm_spec] * 5,
         out_specs=(any_spec, vmem_spec),
         scratch_shapes=[
-            vmem((slices * cy * qx // 128, 128), jnp.int32),
+            vmem((slices * cy * qx // 128 + 8, 128), jnp.int32),
             vmem((2, cy, cx), F32),
             vmem((2, cy, cx), F32),
             vmem((n_il, slices, cy, qx), BF16),

time: 48.1 us -> 48.1 us (level)
  no operation moved by 1% of the time
where the time goes in v7:
time: 48.1 us; the launch traced here: 48 us
  Pallas kernels  45.4 us (94%)
  local copies, waits for them, and re-layouts  1.94 us (4%)
  between operations  0.64 us (1%)
    pallas_call x1, Pallas kernels, on_device(): pl.pallas_call(functools.partial(kernel, dims), out_shape=(pltpu.VMEM((2,...  45.4 us
    unnamed x2, local copies, waits for them, and re-layouts  1.94 us

profile of v7, /device:TPU:1, one launch (start us, length us, event | category | flops | bytes accessed | tf_op | source)
XLA Modules:
  0.0 48.0 jit_solution(11504161349471386413)
XLA Ops:
  0.6 45.4 %shard_map.68 = (f32[2,128,2048]{2,1,0:T(8,128)S(1)}, f32[2,32,128]{2,1,0:T(8,128)S(1)}) custom-call(f32[2,128,2048]{2,1,0:T(8,128)} %bitcast.6, s32[1024,128]{1,0:T(8,128)} %bitcast.7, bf16[2,2048,512]{2,1,0:T(8,128)(2,1)} %constant.6.clone.wx_hbm, bf16[16,2,512,256]{3,2,1,0:T(8,128)(2,1)} %constant.7.clone.ey_hbm, f32[2,16,8,128]{3,2,1,0:T(8,128)} %constant.8.clone.turn_hbm), custom_call_target="tpu_custom_call" | custom-call | tf_op jit(solution)/shard_map/pallas_call | solution.py:615
  46.0 1.3 %copy.9 = f32[1,2,128,2048]{3,2,1,0:T(8,128)} copy(f32[1,2,128,2048]{3,2,1,0:T(8,128)S(1)} %bitcast.4) | data formatting | bytes 4194304
  47.4 0.6 %copy.10 = f32[1,2,32,128]{3,2,1,0:T(8,128)} copy(f32[1,2,32,128]{3,2,1,0:T(8,128)S(1)} %bitcast.5) | data formatting | bytes 65536
